TPU v7x, 128 devices: a whole 4x4x4 slice. The times are simulated.
128 devices in a mesh: lon: 16 (over z, x_hi, core), lat: 8 (over y, x_lo).
Axes of the slice: x: 4 (x_hi: 2, x_lo: 2; x = x_hi * 2 + x_lo), y: 4, z: 4, core: 2. Of those that a mesh axis runs over, the one named last changes fastest.
Arguments:
- tokens: bfloat16 [2, 384, 96, 512], P(None, 'lon', 'lat'), may hold values from -6 to 6
- observed: int32 [2, 384, 96], P(None, 'lon', 'lat'), may hold values 0 or 1
- mask_token: float32 [512], replicated, may hold values from -4 to 4
- gain_one: float32 [512], replicated, may hold values from 0.25 to 1.75
- qkv_one: bfloat16 [512, 1536], replicated, may hold values from -0.25 to 0.25
- table_one: float32 [8, 759], replicated, may hold values from -4 to 408
- proj_one: bfloat16 [512, 512], replicated, may hold values from -0.25 to 0.25
- merge_weight: bfloat16 [2048, 1024], replicated, may hold values from -0.125 to 0.125
- gain_two: float32 [1024], replicated, may hold values from 0.25 to 1.75
- qkv_two: bfloat16 [1024, 3072], replicated, may hold values from -0.1875 to 0.1875
- table_two: float32 [16, 759], replicated, may hold values from -4 to 408
- proj_two: bfloat16 [1024, 1024], replicated, may hold values from -0.1875 to 0.1875
- cotangent: bfloat16 [2, 192, 48, 1024], P(None, 'lon', 'lat'), may hold values from -6 to 6
Outputs:
- result: bfloat16 [2, 192, 48, 1024], P(None, 'lon', 'lat')
- grad_tokens: bfloat16 [2, 384, 96, 512], P(None, 'lon', 'lat')
- grad_qkv_one: float32 [512, 1536], P('lon', 'lat')
- grad_qkv_two: float32 [1024, 3072], P('lon', 'lat')
All inputs are finite; a program needn't handle non-finite values. No bound on the sum of `observed` on one device may be relied on, other than what follows from the above.
Results may differ from a plain program's by a relative error of at most 0.035.
Values may be sent and summed in bfloat16 or wider, within the bound.
A program may use at most 128 MiB of HBM per device.

v0:
```python
import jax
import jax.numpy as jnp
from jax import lax
from jax.sharding import PartitionSpec as P

WV = 2
WL = 12
WA = 6


EPS = 1e-05
NEG = -1000000000.0


def shifted(block, axis, distance):
    devices = range(lax.axis_size(axis))
    route = [((i - distance) % len(devices), i) for i in devices]
    return lax.ppermute(block, axis, route)


def norm_rows(x, gain):
    values = x.astype(jnp.float32)
    centre = jnp.mean(values, axis=-1, keepdims=True)
    spread = jnp.mean((values - centre) ** 2, axis=-1, keepdims=True)
    return ((values - centre) * lax.rsqrt(spread + EPS) * gain).astype(jnp.bfloat16)


def to_windows(x):
    depth, along, across, width = x.shape
    x = x.reshape(depth // WV, WV, along // WL, WL, across // WA, WA, width)
    x = x.transpose(0, 2, 4, 1, 3, 5, 6)
    return x.reshape(-1, WV * WL * WA, width)


def from_windows(blocks, depth, along, across):
    width = blocks.shape[-1]
    blocks = blocks.reshape(depth // WV, along // WL, across // WA, WV, WL, WA, width)
    blocks = blocks.transpose(0, 3, 1, 4, 2, 5, 6)
    return blocks.reshape(depth, along, across, width)


def relative_index():
    grid = jnp.stack(
        jnp.meshgrid(jnp.arange(WV), jnp.arange(WL), jnp.arange(WA), indexing="ij"), -1
    ).reshape(-1, 3)
    offset = grid[:, None, :] - grid[None, :, :]
    return (
        ((offset[..., 0] + WV - 1) * (2 * WL - 1) + offset[..., 1] + WL - 1) * (2 * WA - 1)
        + offset[..., 2]
        + WA
        - 1
    )


def window_core(qkv, latitude, table, heads):
    count, cells, triple = qkv.shape
    width = triple // 3
    head = width // heads
    parts = qkv.reshape(count, cells, 3, heads, head)
    query, key, value = (parts[:, :, 0], parts[:, :, 1], parts[:, :, 2])
    score = jnp.einsum(
        "bnhd,bmhd->bhnm", query, key, preferred_element_type=jnp.float32
    ) * head ** (-0.5)
    score = score + table[:, relative_index()][None]
    apart = jnp.abs(latitude[:, :, None] - latitude[:, None, :]) >= WA
    score = jnp.where(apart[:, None], NEG, score)
    top = jnp.max(score, axis=-1, keepdims=True)
    expo = jnp.exp(score - top)
    weights = (expo / jnp.sum(expo, axis=-1, keepdims=True)).astype(jnp.bfloat16)
    mixed = jnp.einsum("bhnm,bmhd->bnhd", weights, value, preferred_element_type=jnp.float32)
    return mixed.astype(jnp.bfloat16).reshape(count, cells, width)


def roll_into(x):
    half_lon, half_lat = (WL // 2, WA // 2)
    strip = shifted(x[:, :half_lon], "lon", -1)
    x = jnp.concatenate([x[:, half_lon:], strip], axis=1)
    strip = shifted(x[:, :, :half_lat], "lat", -1)
    x = jnp.concatenate([x[:, :, half_lat:], strip], axis=2)
    return x


def roll_out(y):
    half_lon, half_lat = (WL // 2, WA // 2)
    strip = shifted(y[:, :, -half_lat:], "lat", 1)
    y = jnp.concatenate([strip, y[:, :, :-half_lat]], axis=2)
    strip = shifted(y[:, -half_lon:], "lon", 1)
    y = jnp.concatenate([strip, y[:, :-half_lon]], axis=1)
    return y


def reduce_weight(term):
    partial_sum = lax.psum_scatter(
        term.astype(jnp.bfloat16), "lon", scatter_dimension=0, tiled=True
    )
    return lax.psum_scatter(partial_sum, "lat", scatter_dimension=1, tiled=True).astype(jnp.float32)


def level_forward(x, gain, w_qkv, table, w_proj, heads):
    depth, along, across, width = x.shape
    half_lat = WA // 2
    normed = norm_rows(x, gain)
    rolled = roll_into(normed)
    qkv = jnp.dot(rolled, w_qkv, preferred_element_type=jnp.float32).astype(jnp.bfloat16)
    place = lax.axis_index("lat") * across + jnp.arange(across, dtype=jnp.int32)
    line = (place + half_lat) % (across * lax.axis_size("lat"))
    lat_grid = jnp.broadcast_to(line[None, None, :, None], (depth, along, across, 1))
    lat_win = to_windows(lat_grid)[:, :, 0]
    qkv_win = to_windows(qkv)
    mixed = from_windows(window_core(qkv_win, lat_win, table, heads), depth, along, across)
    branch = jnp.dot(mixed, w_proj, preferred_element_type=jnp.float32).astype(jnp.bfloat16)
    branch = roll_out(branch)
    out = (x.astype(jnp.float32) + branch.astype(jnp.float32)).astype(jnp.bfloat16)
    return (out, (rolled, qkv_win, mixed, lat_win))


def level_backward(grad_out, x, saved, gain, w_qkv, table, w_proj, heads):
    rolled, qkv_win, mixed, lat_win = saved
    depth, along, across, width = x.shape
    grad_branch = roll_into(grad_out)
    _, back_proj = jax.vjp(
        lambda m: jnp.dot(m, w_proj, preferred_element_type=jnp.float32).astype(jnp.bfloat16), mixed
    )
    (grad_mixed,) = back_proj(grad_branch)
    _, back_core = jax.vjp(lambda q: window_core(q, lat_win, table, heads), qkv_win)
    (grad_win,) = back_core(to_windows(grad_mixed))
    grad_qkv = from_windows(grad_win, depth, along, across)
    term = jnp.einsum(
        "tc,tk->ck",
        rolled.reshape(-1, width),
        grad_qkv.reshape(-1, 3 * width),
        preferred_element_type=jnp.float32,
    )
    _, back_in = jax.vjp(
        lambda r: jnp.dot(r, w_qkv, preferred_element_type=jnp.float32).astype(jnp.bfloat16), rolled
    )
    (grad_rolled,) = back_in(grad_qkv)
    grad_normed = roll_out(grad_rolled)
    _, back_norm = jax.vjp(lambda z: norm_rows(z, gain), x)
    (grad_inner,) = back_norm(grad_normed)
    grad_x = (grad_out.astype(jnp.float32) + grad_inner.astype(jnp.float32)).astype(jnp.bfloat16)
    return (grad_x, reduce_weight(term))


def merge_patches(x, weight):
    depth, along, across, width = x.shape
    x = x.reshape(depth, along // 2, 2, across // 2, 2, width).transpose(0, 1, 3, 2, 4, 5)
    x = x.reshape(depth, along // 2, across // 2, 4 * width)
    return jnp.dot(x, weight, preferred_element_type=jnp.float32).astype(jnp.bfloat16)


def shards(
    tokens,
    observed,
    mask_token,
    gain_one,
    qkv_one,
    table_one,
    proj_one,
    merge_weight,
    gain_two,
    qkv_two,
    table_two,
    proj_two,
    cotangent,
):
    present = observed[..., None] == 1
    first = jnp.where(present, tokens, mask_token.astype(jnp.bfloat16))
    heads_one = table_one.shape[0]
    heads_two = table_two.shape[0]
    out_one, saved_one = level_forward(first, gain_one, qkv_one, table_one, proj_one, heads_one)
    second, back_merge = jax.vjp(lambda z: merge_patches(z, merge_weight), out_one)
    result, saved_two = level_forward(second, gain_two, qkv_two, table_two, proj_two, heads_two)
    grad_second, grad_qkv_two = level_backward(
        cotangent, second, saved_two, gain_two, qkv_two, table_two, proj_two, heads_two
    )
    (grad_one,) = back_merge(grad_second)
    grad_first, grad_qkv_one = level_backward(
        grad_one, first, saved_one, gain_one, qkv_one, table_one, proj_one, heads_one
    )
    grad_tokens = jnp.where(present, grad_first, jnp.zeros_like(grad_first))
    return (result, grad_tokens, grad_qkv_one, grad_qkv_two)


def solution(mesh):
    return jax.shard_map(
        shards,
        mesh=mesh,
        in_specs=(
            P(None, "lon", "lat", None),
            P(None, "lon", "lat"),
            P(),
            P(),
            P(),
            P(),
            P(),
            P(),
            P(),
            P(),
            P(),
            P(),
            P(None, "lon", "lat", None),
        ),
        out_specs=(
            P(None, "lon", "lat", None),
            P(None, "lon", "lat", None),
            P("lon", "lat"),
            P("lon", "lat"),
        ),
        check_vma=False,
    )
```

profile of v0, /device:TPU:0, one launch (start us, length us, event | category | flops | bytes accessed | tf_op | source)
XLA Modules:
  0.0 613.7 jit_solution(616113027621109646)
XLA Ops:
  13.7 6.0 collective-permute-start
  29.2 38.9 %gather_fusion = f32[20736,8]{1,0:T(8,128)} fusion(f32[8,759]{0,1:T(8,128)S(1)} %copy.96, s32[21504]{0:T(1024)S(1)} %pad_clamp_fusion), kind=kCustom, calls=%fused_computation | custom fusion | bytes 1410048 | tf_op jit(solution)/shard_map/gather | solution.py:64
  68.1 11.2 %copy.97 = f32[144,144,8]{0,1,2:T(8,128)S(1)} copy(f32[144,144,8]{2,1,0:T(8,128)} %bitcast.215) | data formatting | bytes 1327104 | tf_op jit(solution)/shard_map/gather | solution.py:64
  88.7 6.8 %reshape_reshape.13 = bf16[4,144,3,8,64]{4,3,2,0,1:T(8,128)(2,1)} reshape(bf16[1,2,2,2,12,6,1536]{6,2,1,5,4,3,0:T(2,128)(2,1)} %copy.91) | data formatting | bytes 3538944 | tf_op jit(solution)/shard_map/reshape;reshape | solution.py:59
  130.6 5.8 collective-permute-start.8
  155.3 4.2 fusion.172
  162.0 5.0 collective-permute-start.4
  168.7 38.9 %gather_fusion.1 = f32[20736,16]{1,0:T(8,128)} fusion(f32[16,759]{0,1:T(8,128)S(1)} %copy.107, s32[21504]{0:T(1024)S(1)} %pad_clamp_fusion), kind=kCustom, calls=%fused_computation.1 | custom fusion | bytes 2737152 | tf_op jit(solution)/shard_map/gather | solution.py:64
  207.6 12.2 %copy.109 = f32[144,144,16]{0,1,2:T(8,128)} copy(f32[144,144,16]{2,1,0:T(8,128)} %bitcast.213) | data formatting | bytes 2654208 | tf_op jit(solution)/shard_map/gather | solution.py:64
  227.7 6.0 fusion.12
  268.7 4.3 reshape.330
  273.0 5.7 fusion.77
  280.1 8.8 %collective-permute-done.10 = bf16[2,12,3,1024]{3,2,1,0:T(4,128)(2,1)S(1)} collective-permute-done((bf16[2,12,3,1024]{3,2,1,0:T(4,128)(2,1)S(1)}, bf16[2,12,3,1024]{3,2,1,0:T(4,128)(2,1)S(1)}, u32[]{:S(2)}, u32[]{:S(2)}) %collective-permute-start.10) | collective-permute-done | bytes 147488 | tf_op jit(solution)/shard_map/ppermute | solution.py:18
  293.3 4.5 collective-permute-done.11
  326.6 5.0 fusion.7
  339.6 6.6 %copy.130 = bf16[4,144,3,8,64]{4,3,2,0,1:T(8,128)(2,1)} copy(bf16[4,144,3,8,64]{1,4,3,0,2:T(8,128)(2,1)} %pad_add_fusion) | data formatting | bytes 3538944 | tf_op jit(solution)/shard_map/transpose(jvp())/add_any | solution.py:60
  346.2 5.8 reshape.334
  357.8 4.1 convolution_convert_fusion.2
  363.5 6.0 convolution_convert_fusion
  373.1 7.3 %collective-permute-done.14 = bf16[2,24,3,512]{3,1,2,0:T(8,128)(2,1)S(1)} collective-permute-done((bf16[2,24,3,512]{3,1,2,0:T(8,128)(2,1)S(1)}, bf16[2,24,3,512]{3,1,2,0:T(8,128)(2,1)S(1)}, u32[]{:S(2)}, u32[]{:S(2)}) %collective-permute-start.14) | collective-permute-done | bytes 147488 | tf_op jit(solution)/shard_map/ppermute | solution.py:18
  381.6 50.6 %reduce-scatter.9.cloned.1.call-done = bf16[32,1536]{1,0:T(8,128)(2,1)} async-done(((bf16[512,1536]{1,0:T(8,128)(2,1)}), bf16[32,1536]{1,0:T(8,128)(2,1)}) %reduce-scatter.9.cloned.1.call-update) | async-done | bytes 98320 | tf_op jit(solution)/shard_map/reduce_scatter | solution.py:93
  435.4 90.3 %reduce-scatter.11.cloned.1.call-done = bf16[64,3072]{1,0:T(8,128)(2,1)} async-done(((bf16[1024,3072]{1,0:T(8,128)(2,1)}), bf16[64,3072]{1,0:T(8,128)(2,1)}) %reduce-scatter.11.cloned.1.call-update) | async-done | bytes 393232 | tf_op jit(solution)/shard_map/reduce_scatter | solution.py:93
  532.4 32.2 %reduce-scatter.13.cloned.1.call-done = bf16[192,32]{1,0:T(8,128)(2,1)} async-done(((bf16[1536,32]{1,0:T(8,128)(2,1)}), bf16[192,32]{1,0:T(8,128)(2,1)}) %reduce-scatter.13.cloned.1.call-update) | async-done | bytes 12304
  566.1 39.1 %reduce-scatter.15.cloned.1.call-done = bf16[384,64]{1,0:T(8,128)(2,1)} async-done(((bf16[3072,64]{1,0:T(8,128)(2,1)}), bf16[384,64]{1,0:T(8,128)(2,1)}) %reduce-scatter.15.cloned.1.call-update) | async-done | bytes 49168
  (282 shorter events, 193.1 us)
Async XLA Ops:
  7.2 214.7 %copy-start = (bf16[1024,1024]{1,0:T(8,128)(2,1)S(1)}, bf16[1024,1024]{1,0:T(8,128)(2,1)}, u32[]{:S(2)}) copy-start(bf16[1024,1024]{1,0:T(8,128)(2,1)} %param.24) | copy-start | bytes 6291460
  7.2 425.0 %reduce-scatter.9.cloned.1.call-start = ((), (), s32[]{:S(2)}) async-start(), calls=%async_computation.4 | async-start | bytes 1671168 | tf_op jit(solution)/shard_map/reduce_scatter | solution.py:93
  13.7 9.5 %collective-permute-start = (bf16[2,6,12,512]{3,1,2,0:T(8,128)(2,1)}, bf16[2,6,12,512]{3,1,2,0:T(8,128)(2,1)}, u32[]{:S(2)}, u32[]{:S(2)}) collective-permute-start(bf16[2,6,12,512]{3,1,2,0:T(8,128)(2,1)} %slice.184), channel_id=1, source_target_pairs={{8,0},{16,8},{24,16},{32,24},{40,32},{48,40},{56,48},{64,56},{72,6... | collective-permute-start | bytes 442376 | tf_op jit(solution)/shard_map/ppermute | solution.py:18
  24.8 56.2 %collective-permute-start.1 = (bf16[2,24,3,512]{3,1,2,0:T(8,128)(2,1)}, bf16[2,24,3,512]{3,1,2,0:T(8,128)(2,1)}, u32[]{:S(2)}, u32[]{:S(2)}) collective-permute-start(bf16[2,24,3,512]{3,1,2,0:T(8,128)(2,1)} %pad_maximum_fusion.11), channel_id=1, source_target_pairs={{1,0},{2,1},{3,2},{4,3},{5,4},{6,5},{7,6},{0,7},{9,8},{10,9},{11,1... | collective-permute-start | bytes 442376 | tf_op jit(solution)/shard_map/ppermute | solution.py:18
  129.0 8.5 %collective-permute-start.2 = (bf16[2,24,3,512]{3,1,2,0:T(8,128)(2,1)}, bf16[2,24,3,512]{3,1,2,0:T(8,128)(2,1)S(1)}, u32[]{:S(2)}, u32[]{:S(2)}) collective-permute-start(bf16[2,24,3,512]{3,1,2,0:T(8,128)(2,1)} %slice.193), channel_id=1, source_target_pairs={{7,0},{0,1},{1,2},{2,3},{3,4},{4,5},{5,6},{6,7},{15,8},{8,9},{9,10... | collective-permute-start | bytes 442376 | tf_op jit(solution)/shard_map/ppermute | solution.py:18
  130.6 10.2 %collective-permute-start.8 = (bf16[2,6,6,1024]{3,2,1,0:T(8,128)(2,1)}, bf16[2,6,6,1024]{3,2,1,0:T(8,128)(2,1)}, u32[]{:S(2)}, u32[]{:S(2)}) collective-permute-start(bf16[2,6,6,1024]{3,2,1,0:T(8,128)(2,1)} %copy.176), channel_id=1, source_target_pairs={{8,0},{16,8},{24,16},{32,24},{40,32},{48,40},{56,48},{64,56},{72,6... | collective-permute-start | bytes 442376 | tf_op jit(solution)/shard_map/ppermute | solution.py:18
  138.2 9.0 %collective-permute-start.3 = (bf16[2,6,12,512]{3,1,2,0:T(8,128)(2,1)}, bf16[2,6,12,512]{3,1,2,0:T(8,128)(2,1)}, u32[]{:S(2)}, u32[]{:S(2)}) collective-permute-start(bf16[2,6,12,512]{3,1,2,0:T(8,128)(2,1)} %pad_maximum_fusion.9), channel_id=1, source_target_pairs={{120,0},{0,8},{8,16},{16,24},{24,32},{32,40},{40,48},{48,56},{56,6... | collective-permute-start | bytes 442376 | tf_op jit(solution)/shard_map/ppermute | solution.py:18
  142.7 79.1 %collective-permute-start.9 = (bf16[2,12,3,1024]{3,2,1,0:T(4,128)(2,1)}, bf16[2,12,3,1024]{3,2,1,0:T(4,128)(2,1)}, u32[]{:S(2)}, u32[]{:S(2)}) collective-permute-start(bf16[2,12,3,1024]{3,2,1,0:T(4,128)(2,1)} %get-tuple-element.42), channel_id=1, source_target_pairs={{1,0},{2,1},{3,2},{4,3},{5,4},{6,5},{7,6},{0,7},{9,8},{10,9},{11,1... | collective-permute-start | bytes 442376 | tf_op jit(solution)/shard_map/ppermute | solution.py:18
  162.0 57.8 %collective-permute-start.4 = (bf16[2,6,6,1024]{3,2,1,0:T(8,128)(2,1)}, bf16[2,6,6,1024]{3,2,1,0:T(8,128)(2,1)}, u32[]{:S(2)}, u32[]{:S(2)}) collective-permute-start(bf16[2,6,6,1024]{3,2,1,0:T(8,128)(2,1)} %get-tuple-element.48), channel_id=1, source_target_pairs={{8,0},{16,8},{24,16},{32,24},{40,32},{48,40},{56,48},{64,56},{72,6... | collective-permute-start | bytes 442376 | tf_op jit(solution)/shard_map/ppermute | solution.py:18
  221.7 6.0 collective-permute-start.5
  278.9 10.0 %collective-permute-start.10 = (bf16[2,12,3,1024]{3,2,1,0:T(4,128)(2,1)S(1)}, bf16[2,12,3,1024]{3,2,1,0:T(4,128)(2,1)S(1)}, u32[]{:S(2)}, u32[]{:S(2)}) collective-permute-start(bf16[2,12,3,1024]{3,2,1,0:T(4,128)(2,1)S(1)} %get-tuple-element.39), channel_id=1, source_target_pairs={{7,0},{0,1},{1,2},{2,3},{3,4},{4,5},{5,6},{6,7},{15,8},{8,9},{9,10... | collective-permute-start | bytes 442376 | tf_op jit(solution)/shard_map/ppermute | solution.py:18
  280.0 13.1 %collective-permute-start.6 = (bf16[2,12,3,1024]{3,2,1,0:T(4,128)(2,1)S(1)}, bf16[2,12,3,1024]{3,2,1,0:T(4,128)(2,1)S(1)}, u32[]{:S(2)}, u32[]{:S(2)}) collective-permute-start(bf16[2,12,3,1024]{3,2,1,0:T(4,128)(2,1)S(1)} %get-tuple-element.43), channel_id=1, source_target_pairs={{7,0},{0,1},{1,2},{2,3},{3,4},{4,5},{5,6},{6,7},{15,8},{8,9},{9,10... | collective-permute-start | bytes 442376 | tf_op jit(solution)/shard_map/ppermute | solution.py:18
  289.0 8.8 %collective-permute-start.11 = (bf16[2,6,6,1024]{3,2,1,0:T(8,128)(2,1)S(1)}, bf16[2,6,6,1024]{3,2,1,0:T(8,128)(2,1)S(1)}, u32[]{:S(2)}, u32[]{:S(2)}) collective-permute-start(bf16[2,6,6,1024]{3,2,1,0:T(8,128)(2,1)S(1)} %fusion.138), channel_id=1, source_target_pairs={{120,0},{0,8},{8,16},{16,24},{24,32},{32,40},{40,48},{48,56},{56,6... | collective-permute-start | bytes 442376 | tf_op jit(solution)/shard_map/ppermute | solution.py:18
  293.2 8.8 %collective-permute-start.7 = (bf16[2,6,6,1024]{3,2,1,0:T(8,128)(2,1)S(1)}, bf16[2,6,6,1024]{3,2,1,0:T(8,128)(2,1)S(1)}, u32[]{:S(2)}, u32[]{:S(2)}) collective-permute-start(bf16[2,6,6,1024]{3,2,1,0:T(8,128)(2,1)S(1)} %fusion.140), channel_id=1, source_target_pairs={{120,0},{0,8},{8,16},{16,24},{24,32},{32,40},{40,48},{48,56},{56,6... | collective-permute-start | bytes 442376 | tf_op jit(solution)/shard_map/ppermute | solution.py:18
  306.4 3.3 collective-permute-start.12
  310.4 5.5 collective-permute-start.13
  362.0 163.7 %reduce-scatter.11.cloned.1.call-start = ((), (), s32[]{:S(2)}) async-start(), calls=%async_computation.5 | async-start | bytes 6684672 | tf_op jit(solution)/shard_map/reduce_scatter | solution.py:93
  369.5 195.1 %reduce-scatter.13.cloned.1.call-start = ((), (), s32[]{:S(2)}) async-start(), calls=%async_computation.6 | async-start | bytes 442368
  373.0 61.1 %copy-start.37 = (f32[2,24,12]{1,2,0:T(8,128)S(1)}, f32[2,24,12]{1,2,0:T(8,128)}, u32[]{:S(2)}) copy-start(f32[2,24,12]{1,2,0:T(8,128)} %copy-done.36) | copy-start | bytes 6916
  373.0 7.4 %collective-permute-start.14 = (bf16[2,24,3,512]{3,1,2,0:T(8,128)(2,1)S(1)}, bf16[2,24,3,512]{3,1,2,0:T(8,128)(2,1)S(1)}, u32[]{:S(2)}, u32[]{:S(2)}) collective-permute-start(bf16[2,24,3,512]{3,1,2,0:T(8,128)(2,1)S(1)} %slice.218), channel_id=1, source_target_pairs={{7,0},{0,1},{1,2},{2,3},{3,4},{4,5},{5,6},{6,7},{15,8},{8,9},{9,10... | collective-permute-start | bytes 442376 | tf_op jit(solution)/shard_map/ppermute | solution.py:18
  380.4 53.6 %collective-permute-start.15 = (bf16[2,6,12,512]{3,1,2,0:T(8,128)(2,1)S(1)}, bf16[2,6,12,512]{3,1,2,0:T(8,128)(2,1)S(1)}, u32[]{:S(2)}, u32[]{:S(2)}) collective-permute-start(bf16[2,6,12,512]{3,1,2,0:T(8,128)(2,1)S(1)} %pad_maximum_fusion.6), channel_id=1, source_target_pairs={{120,0},{0,8},{8,16},{16,24},{24,32},{32,40},{40,48},{48,56},{56,6... | collective-permute-start | bytes 442376 | tf_op jit(solution)/shard_map/ppermute | solution.py:18
  380.5 147.5 %copy-start.42 = (f32[2,24,12]{1,2,0:T(8,128)S(1)}, f32[2,24,12]{1,2,0:T(8,128)}, u32[]{:S(2)}) copy-start(f32[2,24,12]{1,2,0:T(8,128)} %copy-done.41) | copy-start | bytes 6916
  434.0 171.3 %reduce-scatter.15.cloned.1.call-start = ((), (), s32[]{:S(2)}) async-start(), calls=%async_computation.7 | async-start | bytes 884736
  525.7 81.2 %copy-start.1 = (bf16[1024,1024]{1,0:T(8,128)(2,1)S(1)}, bf16[1024,1024]{1,0:T(8,128)(2,1)}, u32[]{:S(2)}) copy-start(bf16[1024,1024]{1,0:T(8,128)(2,1)} %param.24) | copy-start | bytes 6291460
  (49 other events, 393.0 us)
Sparse Core Ops, SparseCore 0:
  362.1 69.9 reduce-scatter.8
  436.9 88.7 reduce-scatter.10
  528.1 36.4 reduce-scatter.12
  567.0 38.2 reduce-scatter.14
where the time goes:
time: 618 us; the launch traced here: 614 us
  waiting for transfers between devices  249 us (40%)
  local copies, waits for them, and re-layouts  214 us (35%)
  matrix products  65.5 us (11%)
  other arithmetic  42.4 us (7%)
  starting transfers between devices  27.8 us (4%)
  between operations  15.1 us (2%)
    reduce_scatter x2, waiting for transfers between devices, reduce_weight(): lax.psum_scatter(term.astype(jnp.bfloat16), 'lon', scatter_dimension=0, t...  141 us
    gather x4, local copies, waits for them, and re-layouts, window_core(): score = score + table[:, relative_index()][None]  101 us
    unnamed x6, waiting for transfers between devices  71.4 us
    ppermute x16, waiting for transfers between devices, shifted(): return lax.ppermute(block, axis, route)  37 us
    unnamed x121, local copies, waits for them, and re-layouts  32.4 us
    ppermute x16, starting transfers between devices, shifted(): return lax.ppermute(block, axis, route)  27.4 us
    dot_general x6, matrix products, window_core(): jnp.einsum('bhnm,bmhd->bnhd', weights, value, preferred_element_type=jnp....  12.7 us
    dot_general x6, matrix products, window_core(): jnp.einsum('bnhd,bmhd->bhnm', query, key, preferred_element_type=jnp.floa...  12.6 us
  transfers between devices with their start and end apart: 20, of which 15 were waited for; matrix products, arithmetic and copies ran while one was open for 26% of the time, Pallas kernels for 0%

commit v1 on v0

v1 whole, which is shorter than its diff:
```python
import functools
from types import SimpleNamespace
import numpy as np
import jax
import jax.numpy as jnp
from jax import lax
from jax.experimental import pallas as pl
from jax.experimental.pallas import tpu as pltpu
from jax.sharding import PartitionSpec as P

BF = jnp.bfloat16
F32 = jnp.float32
EPS = 1e-05
NEG = -1000000000.0
MESH = pl.DeviceIdType.MESH
CELLS = 144
HALF = 72

SEG1 = ((0, 336), (336, 112), (448, 112), (560, 48))
SEG2 = ((0, 48), (48, 48), (96, 48), (144, 48))


def _cells(along, across, half_lon, half_lat):
    out = [[], [], [], []]
    for v in range(2):
        for i in range(along):
            for j in range(across):
                seg = (1 if i < half_lon else 0) + (2 if j < half_lat else 0)
                moved = (v, (i - half_lon) % along, (j - half_lat) % across)
                out[seg].append(((v, i, j), moved))
    return out


def _send_index(segs, cells, row_of):
    out = [-1] * (segs[-1][0] + segs[-1][1])
    for (start, _), members in zip(segs, cells):
        for n, (cell, _) in enumerate(members):
            out[start + n] = row_of(*cell)
    return out


def _recv_index(segs, cells, row_of, rows):
    out = [-1] * rows
    for (start, _), members in zip(segs, cells):
        for n, (_, moved) in enumerate(members):
            out[row_of(*moved)] = start + n
    return out


def _inverse(index, rows):
    out = [-1] * rows
    for n, m in enumerate(index):
        if m >= 0:
            out[m] = n
    return out


def _nat1(v, i, j):
    return (v * 12 + j) * 24 + i


def _win1(v, i, j):
    return ((i // 12) * 2 + j // 6) * CELLS + (j % 6) * 24 + v * 12 + i % 12


def _merge(v, i, j):
    return ((i % 2) * 2 + j % 2) * CELLS + (j // 2) * 24 + v * 12 + i // 2


def _nat2(v, i, j):
    return (i * 6 + j) * 2 + v


def _win2(v, i, j):
    return j * 24 + v * 12 + i


def _indices():
    one = _cells(24, 12, 6, 3)
    two = _cells(12, 6, 6, 3)
    s1 = _send_index(SEG1, one, _nat1)
    r1 = _recv_index(SEG1, one, _win1, 576)
    s2 = _send_index(SEG1, one, _win1)
    r2 = _recv_index(SEG1, one, _merge, 576)
    sc = _send_index(SEG2, two, _nat2)
    rc = _recv_index(SEG2, two, _win2, CELLS)
    flip = [-1] * 768
    for x in range(3):
        for y in range(23):
            for z in range(11):
                flip[((2 - x) * 23 + 22 - y) * 11 + 10 - z] = z * 69 + x * 23 + y
    pick = [-1] * 768
    for z in range(11):
        for v in range(2):
            for l in range(12):
                pick[z * 69 + v * 23 + l] = z * 24 + v * 12 + l
    return dict(s1=s1, r1=r1, s2=s2, r2=r2, s3=_inverse(r2, 608), r3=_inverse(s2, 576), s4=_inverse(r1, 608),
                r4=_inverse(s1, 576), sc=sc, rc=rc, sr=_inverse(rc, 192), rr=_inverse(sc, CELLS), flip=flip, pick=pick)


INDEX = _indices()
TABLE_OF = np.full((768, len(INDEX)), -1, np.int32)
for _n, _rows in enumerate(INDEX.values()):
    TABLE_OF[:len(_rows), _n] = _rows

SHAPES = dict(first=(576, 512), cot=(CELLS, 1024), w1=(512, 1536), p1=(512, 512), p2=(1024, 1024),
              wm=(2048, 1024), w2=(1024, 3072))
LOADS = tuple(SHAPES)


def nn(a, b):
    return lax.dot_general(a, b, (((1,), (0,)), ((), ())), preferred_element_type=F32)


def nt(a, b):
    return lax.dot_general(a, b, (((1,), (1,)), ((), ())), preferred_element_type=F32)


def tn(a, b):
    return lax.dot_general(a, b, (((0,), (0,)), ((), ())), preferred_element_type=F32)


def norm_stats(x):
    centre = jnp.mean(x, axis=-1, keepdims=True)
    dev = x - centre
    spread = jnp.mean(dev * dev, axis=-1, keepdims=True)
    return dev, lax.rsqrt(spread + EPS)


def loop(n, body):
    lax.fori_loop(0, n, lambda i, c: (body(i), c)[1], 0)


SCRATCH = dict(
    {k: pltpu.VMEM(SHAPES[k], BF) for k in LOADS},
    parts=pltpu.VMEM((72, 768), F32),
    ext=pltpu.VMEM((24, 24, 264), F32),
    bias=pltpu.VMEM((24, CELLS, CELLS), F32),
    madd=pltpu.VMEM((2, CELLS, CELLS), F32),
    xr=pltpu.VMEM((4, 608, 512), BF),
    xs=pltpu.VMEM((4, 272, 512), BF),
    cr=pltpu.VMEM((2, 192, 1024), BF),
    cs=pltpu.VMEM((2, 144, 1024), BF),
    x1=pltpu.VMEM((576, 512), BF),
    rolled1=pltpu.VMEM((576, 512), BF),
    rolled1t=pltpu.VMEM((512, 576), BF),
    qkv1=pltpu.VMEM((576, 1536), BF),
    dqkv1=pltpu.VMEM((576, 1536), BF),
    prob1=pltpu.VMEM((16, 288, CELLS), BF),
    mixed1=pltpu.VMEM((576, 512), BF),
    out1=pltpu.VMEM((576, 512), BF),
    gm1=pltpu.VMEM((576, 512), BF),
    g1=pltpu.VMEM((576, 512), BF),
    merged=pltpu.VMEM((576, 512), BF),
    second=pltpu.VMEM((CELLS, 1024), BF),
    rolled2=pltpu.VMEM((CELLS, 1024), BF),
    qkv2=pltpu.VMEM((CELLS, 3072), BF),
    dqkv2=pltpu.VMEM((2, CELLS, 3072), BF),
    half2=pltpu.VMEM((2, CELLS, 512), BF),
    theirs2=pltpu.VMEM((CELLS, 512), BF),
    halft=pltpu.VMEM((2, 512, CELLS), BF),
    prob2=pltpu.VMEM((8, 288, CELLS), BF),
    mixed2=pltpu.VMEM((CELLS, 1024), BF),
    ct=pltpu.VMEM((CELLS, 1024), BF),
    gm2=pltpu.VMEM((CELLS, 1024), BF),
    res=pltpu.VMEM((CELLS, 1024), BF),
    gs=pltpu.VMEM((CELLS, 1024), BF),
    b2=pltpu.VMEM((3, 64, 64, 128), BF),
    b2r0=pltpu.VMEM((3, 3, 16, 64, 128), BF),
    b2r1=pltpu.VMEM((3, 3, 4, 64, 128), BF),
    b2r2=pltpu.VMEM((3, 3, 1, 64, 128), BF),
    b1=pltpu.VMEM((2, 3, 64, 16, 128), BF),
    b1c=pltpu.VMEM((3, 64, 16, 128), BF),
    b1r0=pltpu.VMEM((3, 3, 16, 16, 128), BF),
    b1r1=pltpu.VMEM((3, 3, 4, 16, 128), BF),
    b1r2=pltpu.VMEM((3, 3, 1, 16, 128), BF),
    load_sem=pltpu.SemaphoreType.DMA((len(LOADS),)),
    halo_send=pltpu.SemaphoreType.DMA((18,)),
    halo_recv=pltpu.SemaphoreType.DMA((18,)),
    rs_send=pltpu.SemaphoreType.DMA((54,)),
    rs_recv=pltpu.SemaphoreType.DMA((54,)),
    core_send=pltpu.SemaphoreType.DMA((3,)),
    core_recv=pltpu.SemaphoreType.DMA((3,)),
)
SMALL = ("index", "seen", "mask", "table", "gain1", "gain2")
OUTPUTS = ("o_res", "o_tok", "o_q1", "o_q2")

ORDERS = (("z", "x", "y"), ("x", "y", "z"), ("y", "z", "x"))


def body(sizes, *refs):
    n_lon, n_lat = sizes
    names = ["in_" + n for n in LOADS + SMALL] + list(OUTPUTS) + list(SCRATCH)
    R = SimpleNamespace(**dict(zip(names, refs, strict=True)))

    e = lax.axis_index("lon")
    d = lax.axis_index("lat")
    core, xh, z = lax.rem(e, 2), lax.rem(e // 2, 2), e // 4
    xl, y = lax.rem(d, 2), d // 2
    x = xh * 2 + xl
    place = dict(x=x, y=y, z=z)
    e_up, e_dn = lax.rem(e + 1, n_lon), lax.rem(e + n_lon - 1, n_lon)
    d_up, d_dn = lax.rem(d + 1, n_lat), lax.rem(d + n_lat - 1, n_lat)
    last = d == n_lat - 1
    ahead = ((e_up, d), (e, d_up), (e_up, d_up))
    behind = ((e_dn, d), (e, d_dn), (e_dn, d_dn))
    other = (e + 1 - 2 * core, d)

    def device(x, y, z):
        return (z * 4 + (x // 2) * 2 + core, y * 2 + lax.rem(x, 2))

    def along(axis, k):
        at = dict(place)
        at[axis] = lax.rem(at[axis] + k, 4)
        return device(**at)

    loads = SimpleNamespace()
    for n, name in enumerate(LOADS):
        copy = pltpu.make_async_copy(getattr(R, "in_" + name), getattr(R, name), R.load_sem.at[n])
        copy.start()
        setattr(loads, name, copy)

    barrier = pltpu.get_barrier_semaphore()
    partners = list(ahead) + list(behind) + [other]
    for axis in place:
        for k in (1, 2, 3):
            partners.append(along(axis, k))
    for who in partners:
        pl.semaphore_signal(barrier, inc=1, device_id=who, device_id_type=MESH)
    pl.semaphore_wait(barrier, len(partners))

    def exchange(n, segs, source, target, to):
        copies = []
        for k in range(3):
            start, size = segs[k + 1]
            rows = pl.ds(start, size)
            copies.append(pltpu.make_async_remote_copy(
                src_ref=source.at[pl.ds(start - segs[0][1], size)],
                dst_ref=target.at[rows],
                send_sem=R.halo_send.at[3 * n + k],
                recv_sem=R.halo_recv.at[3 * n + k],
                device_id=to[k],
                device_id_type=MESH))
        for c in copies:
            c.start()
        return copies

    def wait(copies):
        for c in copies:
            c.wait()

    def take(key, start, size, columns):
        n = list(INDEX).index(key)
        col = R.in_index[pl.ds(start, size), n:n + 1]
        hit = col == lax.broadcasted_iota(jnp.int32, (size, columns), 1)
        return jnp.where(hit, 1.0, 0.0).astype(BF)

    row = lax.broadcasted_iota(jnp.int32, (576, 24), 0)
    col = lax.broadcasted_iota(jnp.int32, (576, 24), 1)
    per = nn(jnp.where(row // 24 == col, 1.0, 0.0).astype(BF), R.in_seen[...].astype(F32).astype(BF))
    present = jnp.sum(jnp.where(lax.rem(row, 24) == col, per, 0.0), axis=-1, keepdims=True) > 0.5

    loads.first.wait()
    R.first[...] = jnp.where(present, R.first[...].astype(F32), R.in_mask[...].astype(BF).astype(F32)).astype(BF)
    R.xs[0] = nn(take("s1", 336, 272, 576), R.first[...]).astype(BF)
    halo0 = exchange(0, SEG1, R.xs.at[0], R.xr.at[0], behind)
    R.xr[0, 0:336] = nn(take("s1", 0, 336, 576), R.first[...]).astype(BF)
    loads.cot.wait()
    R.cs[0] = nn(take("sc", 48, 144, CELLS), R.cot[...]).astype(BF)
    halo_c = exchange(4, SEG2, R.cs.at[0], R.cr.at[0], behind)
    R.cr[0, 0:48] = nn(take("sc", 0, 48, CELLS), R.cot[...]).astype(BF)

    table = R.in_table[...]
    high = table.astype(BF).astype(F32)
    mid = (table - high).astype(BF).astype(F32)
    low = table - high - mid
    parts = jnp.concatenate([high, mid, low], axis=0).astype(BF)
    R.parts[...] = nn(parts, take("flip", 0, 768, 768))
    picked = take("pick", 0, 768, 264)
    for v in range(2):
        for l in range(12):
            shift = (1 - v) * 23 + 11 - l
            moved = pltpu.roll(R.parts[...], (768 - shift) % 768, 1) if shift else R.parts[...]
            got = nn(moved.astype(BF), picked)
            R.ext[:, v * 12 + l, :] = got[0:24] + got[24:48] + got[48:72]
    rows = lax.broadcasted_iota(jnp.int32, (CELLS, CELLS), 0)
    cols = lax.broadcasted_iota(jnp.int32, (CELLS, CELLS), 1)
    apart = jnp.logical_xor(rows < HALF, cols < HALF)
    apart_add = jnp.where(apart, NEG, 0.0).astype(F32) * jnp.where(last, 1.0, 0.0).astype(F32)
    R.madd[0] = jnp.zeros((CELLS, CELLS), F32)
    R.madd[1] = apart_add

    def expand(h):
        for a in range(6):
            piece = R.ext[h, :, (5 - a) * 24:(5 - a) * 24 + CELLS]
            R.bias[h, a * 24:(a + 1) * 24, :] = piece

    def expand_masked(h):
        expand(8 + h)
        R.bias[8 + h] = R.bias[8 + h] + R.madd[1]

    loop(8, expand)

    lane = lax.broadcasted_iota(jnp.int32, (1, 128), 1)
    left = jnp.where(lane < 64, 1.0, 0.0).astype(BF)
    right = jnp.where(lane < 64, 0.0, 1.0).astype(BF)
    is_left = lax.broadcasted_iota(jnp.int32, (CELLS, 128), 1) < 64

    def stack(t):
        return jnp.concatenate([t * left, t * right], axis=0)

    def attend(qkv, prob, mixed, unit, rows, pair, width, bias):
        at = lambda part: pl.ds(pl.multiple_of(part * width + pair * 128, 128), 128)
        q = qkv[rows, at(0)] * BF(0.125)
        k = qkv[rows, at(1)]
        v = qkv[rows, at(2)]
        score = nt(stack(q), k) + bias
        top = jnp.max(score, axis=-1, keepdims=True)
        expo = jnp.exp(score - top)
        p = (expo * (1.0 / jnp.sum(expo, axis=-1, keepdims=True))).astype(BF)
        prob[unit] = p
        o = nn(p, v)
        mixed[rows, at(0)] = jnp.where(is_left, o[:CELLS], o[CELLS:]).astype(BF)

    def attend_back(qkv, prob, grad, out, unit, rows, pair, width):
        at = lambda part: pl.ds(pl.multiple_of(part * width + pair * 128, 128), 128)
        q = qkv[rows, at(0)] * BF(0.125)
        k = qkv[rows, at(1)]
        v = qkv[rows, at(2)]
        go = stack(grad[rows, at(0)])
        pb = prob[unit]
        p = pb.astype(F32)
        gw = nt(go, v)
        gs = (p * (gw - jnp.sum(p * gw, axis=-1, keepdims=True))).astype(BF)
        gq = nn(gs, k)
        out[rows, at(0)] = (jnp.where(is_left, gq[:CELLS], gq[CELLS:]) * 0.125).astype(BF)
        out[rows, at(1)] = tn(gs, stack(q)).astype(BF)
        out[rows, at(2)] = tn(pb, go).astype(BF)

    wait(halo0)
    gain1 = R.in_gain1[...]

    def norm1(w):
        rows = pl.ds(pl.multiple_of(w * CELLS, 16), CELLS)
        t = nn(take("r1", pl.multiple_of(w * CELLS, 16), CELLS, 608), R.xr[0])
        R.x1[rows, :] = t.astype(BF)
        dev, inv = norm_stats(t)
        R.rolled1[rows, :] = (dev * inv * gain1).astype(BF)

    loop(4, norm1)
    loads.w1.wait()

    def qkv1(n):
        c = pl.ds(pl.multiple_of(n * 256, 256), 256)
        R.qkv1[:, c] = nn(R.rolled1[...], R.w1[:, c]).astype(BF)

    loop(6, qkv1)

    def fwd1(u):
        pair, w = u // 4, lax.rem(u, 4)
        rows = pl.ds(pl.multiple_of(w * CELLS, 16), CELLS)
        bias = R.bias[pl.ds(pair * 2, 2)] + R.madd[lax.rem(w, 2)][None]
        attend(R.qkv1, R.prob1, R.mixed1, u, rows, pair, 512, bias.reshape(288, CELLS))

    loop(16, fwd1)
    loads.p1.wait()

    def proj1(w):
        rows = pl.ds(pl.multiple_of(w * CELLS, 16), CELLS)
        branch = nn(R.mixed1[rows, :], R.p1[...]).astype(BF).astype(F32)
        R.out1[rows, :] = (R.x1[rows, :].astype(F32) + branch).astype(BF)

    loop(4, proj1)

    R.xs[1] = nn(take("s2", 336, 272, 576), R.out1[...]).astype(BF)
    halo1 = exchange(1, SEG1, R.xs.at[1], R.xr.at[1], behind)
    R.xr[1, 0:336] = nn(take("s2", 0, 336, 576), R.out1[...]).astype(BF)
    loop(16, expand_masked)
    wait(halo_c)
    R.ct[...] = nn(take("rc", 0, CELLS, 192), R.cr[0]).astype(BF)
    loads.p2.wait()

    def grad_mixed2(n):
        c = pl.ds(pl.multiple_of(n * 256, 256), 256)
        R.gm2[:, c] = nt(R.ct[...], R.p2[c, :]).astype(BF)

    loop(4, grad_mixed2)
    R.rolled1t[...] = R.rolled1[...].T
    wait(halo1)
    R.merged[...] = nn(take("r2", 0, 576, 608), R.xr[1]).astype(BF)
    loads.wm.wait()
    acc = nn(R.merged[0:CELLS, :], R.wm[0:512, :])
    for s in range(1, 4):
        acc = acc + nn(R.merged[s * CELLS:(s + 1) * CELLS, :], R.wm[s * 512:(s + 1) * 512, :])
    second = acc.astype(BF)
    R.second[...] = second
    gain2 = R.in_gain2[...]
    dev, inv = norm_stats(second.astype(F32))
    rolled2 = (dev * inv * gain2).astype(BF)
    R.rolled2[...] = rolled2
    loads.w2.wait()

    def qkv2(n):
        c = pl.ds(pl.multiple_of(n * 512, 512), 512)
        R.qkv2[:, c] = nn(R.rolled2[...], R.w2[:, c]).astype(BF)

    loop(6, qkv2)

    r2f = rolled2.astype(F32)
    for t in range(4):
        a = r2f[:, t * 256:t * 256 + 128]
        b = r2f[:, t * 256 + 128:t * 256 + 256]
        c = slice(t * 128, t * 128 + 128)
        R.half2[0, :, c] = jnp.where(is_left, a, pltpu.roll(b, 64, 1)).astype(BF)
        R.half2[1, :, c] = jnp.where(is_left, pltpu.roll(a, 64, 1), b).astype(BF)
    core0 = pltpu.make_async_remote_copy(
        src_ref=R.half2.at[1 - core], dst_ref=R.theirs2, send_sem=R.core_send.at[0],
        recv_sem=R.core_recv.at[0], device_id=other, device_id_type=MESH)
    core0.start()

    everyrow = pl.ds(0, CELLS)

    def fwd2(u):
        bias = R.bias[pl.ds(8 + u * 2, 2)].reshape(288, CELLS)
        attend(R.qkv2, R.prob2, R.mixed2, u, everyrow, u, 1024, bias)
        attend_back(R.qkv2, R.prob2, R.gm2, R.dqkv2.at[0], u, everyrow, u, 1024)

    loop(8, fwd2)
    core1 = pltpu.make_async_remote_copy(
        src_ref=R.dqkv2.at[0], dst_ref=R.dqkv2.at[1], send_sem=R.core_send.at[1],
        recv_sem=R.core_recv.at[1], device_id=other, device_id_type=MESH)
    core1.start()

    grad_rolled = nt(R.dqkv2[0, :, 0:1024], R.w2[:, 0:1024])
    grad_rolled = grad_rolled + nt(R.dqkv2[0, :, 1024:2048], R.w2[:, 1024:2048])
    grad_rolled = grad_rolled + nt(R.dqkv2[0, :, 2048:3072], R.w2[:, 2048:3072])

    def norm_back(grad, xin, gain, grad_out):
        grad = grad.astype(BF).astype(F32) * gain
        dev, inv = norm_stats(xin.astype(F32))
        hat = dev * inv
        inner = inv * (grad - jnp.mean(grad, axis=-1, keepdims=True)
                       - hat * jnp.mean(grad * hat, axis=-1, keepdims=True))
        return (grad_out.astype(F32) + inner.astype(BF).astype(F32)).astype(BF)

    R.gs[...] = norm_back(grad_rolled, R.second[...], gain2, R.ct[...])
    for s in range(4):
        R.merged[s * CELLS:(s + 1) * CELLS, :] = nt(R.gs[...], R.wm[s * 512:(s + 1) * 512, :]).astype(BF)
    R.xs[2] = nn(take("s3", 336, 272, 576), R.merged[...]).astype(BF)
    halo2 = exchange(2, SEG1, R.xs.at[2], R.xr.at[2], ahead)
    R.xr[2, 0:336] = nn(take("s3", 0, 336, 576), R.merged[...]).astype(BF)

    branch = nn(R.mixed2[...], R.p2[...]).astype(BF).astype(F32)
    R.res[...] = (R.second[...].astype(F32) + branch).astype(BF)
    R.cs[1] = nn(take("sr", 48, 144, CELLS), R.res[...]).astype(BF)
    halo_r = exchange(5, SEG2, R.cs.at[1], R.cr.at[1], ahead)
    R.cr[1, 0:48] = nn(take("sr", 0, 48, CELLS), R.res[...]).astype(BF)

    R.halft[0] = R.half2[core].T
    core0.wait()
    R.halft[1] = R.theirs2[...].T
    core1.wait()

    def term2(t):
        c = pl.ds(pl.multiple_of(t * 384, 128), 384)
        g = nn(R.halft[0], R.dqkv2[0, :, c]) + nn(R.halft[1], R.dqkv2[1, :, c])
        g = g.astype(BF)
        yy, xx = t // 2, lax.rem(t, 2)
        for zz in range(4):
            for hh in range(2):
                r = (zz * 2 + hh) * 64
                at = dict(z=zz, x=hh * 2 + xx, y=yy)
                for p, order in enumerate(ORDERS):
                    block = (at[order[0]] * 4 + at[order[1]]) * 4 + at[order[2]]
                    R.b2[p, block] = g[r:r + 64, p * 128:(p + 1) * 128]

    loop(8, term2)

    def rs_start(buf, recv, sem0, step):
        copies = []
        for p, order in enumerate(ORDERS):
            base = 0
            for s in range(step):
                base = base + place[order[s]] * (16 >> (2 * s))
            size = 16 >> (2 * step)
            axis = order[step]
            for k in (1, 2, 3):
                to = lax.rem(place[axis] + k, 4)
                n = sem0 + (step * 3 + p) * 3 + k - 1
                copies.append(pltpu.make_async_remote_copy(
                    src_ref=buf.at[p, pl.ds(base + to * size, size)],
                    dst_ref=recv.at[p, k - 1],
                    send_sem=R.rs_send.at[n],
                    recv_sem=R.rs_recv.at[n],
                    device_id=along(axis, k),
                    device_id_type=MESH))
        for c in copies:
            c.start()
        return copies

    def rs_add(buf, recv, step, copies):
        wait(copies)
        size = 16 >> (2 * step)
        for p, order in enumerate(ORDERS):
            base = 0
            for s in range(step + 1):
                base = base + place[order[s]] * (16 >> (2 * s))

            def add(b):
                t = buf[p, base + b].astype(F32) + recv[p, 0, b].astype(F32)
                t = t + recv[p, 1, b].astype(F32) + recv[p, 2, b].astype(F32)
                buf[p, base + b] = t.astype(BF)

            loop(size, add)

    def rs_last(buf, recv, p, copies):
        order = ORDERS[p]
        base = (place[order[0]] * 4 + place[order[1]]) * 4 + place[order[2]]
        t = buf[p, base].astype(F32) + recv[p, 0, 0].astype(F32)
        return t + recv[p, 1, 0].astype(F32) + recv[p, 2, 0].astype(F32)

    big = rs_start(R.b2, R.b2r0, 0, 0)

    wait(halo2)
    R.g1[...] = nn(take("r3", 0, 576, 608), R.xr[2]).astype(BF)

    def grad_mixed1(w):
        rows = pl.ds(pl.multiple_of(w * CELLS, 16), CELLS)
        R.gm1[rows, :] = nt(R.g1[rows, :], R.p1[...]).astype(BF)

    loop(4, grad_mixed1)

    def bwd1(u):
        pair, w = u // 4, lax.rem(u, 4)
        rows = pl.ds(pl.multiple_of(w * CELLS, 16), CELLS)
        attend_back(R.qkv1, R.prob1, R.gm1, R.dqkv1, u, rows, pair, 512)

    loop(16, bwd1)

    def term1(t):
        c = pl.ds(pl.multiple_of(t * 384, 128), 384)
        g = nn(R.rolled1t[...], R.dqkv1[:, c])
        for zz in range(4):
            for hh in range(2):
                for cc in range(2):
                    r = ((zz * 2 + hh) * 2 + cc) * 32
                    upper = g[r:r + 16, 128:256]
                    lower = pltpu.roll(g[r + 16:r + 32, 128:256], 64, 1)
                    pick = is_left[0:16]
                    mixes = (jnp.where(pick, upper, lower), jnp.where(pick, lower, upper))
                    for odd in range(2):
                        at = dict(z=zz, x=hh * 2 + odd, y=t)
                        lanes = slice(odd * 256, odd * 256 + 128)
                        pieces = (g[r:r + 16, lanes], g[r + 16:r + 32, lanes], mixes[odd])
                        for p, order in enumerate(ORDERS):
                            block = (at[order[0]] * 4 + at[order[1]]) * 4 + at[order[2]]
                            R.b1[cc, p, block] = pieces[p].astype(BF)

    loop(4, term1)
    core2 = pltpu.make_async_remote_copy(
        src_ref=R.b1.at[1 - core], dst_ref=R.b1c, send_sem=R.core_send.at[2],
        recv_sem=R.core_recv.at[2], device_id=other, device_id_type=MESH)
    core2.start()
    rs_add(R.b2, R.b2r0, 0, big)
    big = rs_start(R.b2, R.b2r1, 0, 1)

    core2.wait()
    mine = R.b1.at[core]

    def add_core(b):
        for p in range(3):
            mine[p, b] = (mine[p, b].astype(F32) + R.b1c[p, b].astype(F32)).astype(BF)

    loop(64, add_core)
    small = rs_start(mine, R.b1r0, 27, 0)

    def tail1(w):
        rows = pl.ds(pl.multiple_of(w * CELLS, 16), CELLS)
        grad = nt(R.dqkv1[rows, :], R.w1[...])
        R.out1[rows, :] = norm_back(grad, R.x1[rows, :], gain1, R.g1[rows, :])

    loop(4, tail1)
    R.xs[3] = nn(take("s4", 336, 272, 576), R.out1[...]).astype(BF)
    halo3 = exchange(3, SEG1, R.xs.at[3], R.xr.at[3], ahead)
    R.xr[3, 0:336] = nn(take("s4", 0, 336, 576), R.out1[...]).astype(BF)

    rs_add(mine, R.b1r0, 0, small)
    small = rs_start(mine, R.b1r1, 27, 1)
    rs_add(R.b2, R.b2r1, 1, big)
    big = rs_start(R.b2, R.b2r2, 0, 2)
    wait(halo_r)
    R.o_res[...] = nn(take("rr", 0, CELLS, 192), R.cr[1]).astype(BF)
    rs_add(mine, R.b1r1, 1, small)
    small = rs_start(mine, R.b1r2, 27, 2)
    wait(halo3)
    R.o_tok[...] = jnp.where(present, nn(take("r4", 0, 576, 608), R.xr[3]), 0.0).astype(BF)
    wait(big)
    for p in range(3):
        R.o_q2[:, p * 128:(p + 1) * 128] = rs_last(R.b2, R.b2r2, p, big)
    wait(small)
    a, b, m = [rs_last(mine, R.b1r2, p, small) for p in range(3)]
    turned = pltpu.roll(m, 64, 1)
    even = xl == 0
    a_turned = pltpu.roll(a, 64, 1)
    b_turned = pltpu.roll(b, 64, 1)
    pick = is_left[0:16]
    R.o_q1[0:16, 0:128] = jnp.where(even, a, jnp.where(pick, turned, a_turned))
    R.o_q1[16:32, 0:128] = jnp.where(even, b, jnp.where(pick, m, b_turned))
    R.o_q1[0:16, 128:192] = jnp.where(even, m, a_turned)[:, 0:64]
    R.o_q1[16:32, 128:192] = jnp.where(even, turned, b_turned)[:, 0:64]


def shards(tokens, observed, mask_token, gain_one, qkv_one, table_one, proj_one, merge_weight, gain_two, qkv_two,
           table_two, proj_two, cotangent, sizes):
    first = tokens.transpose(0, 2, 1, 3).reshape(576, 512)
    cot = cotangent.transpose(1, 2, 0, 3).reshape(CELLS, 1024)
    seen = observed.transpose(0, 2, 1).reshape(24, 24)
    table = jnp.pad(jnp.concatenate([table_one, table_two], axis=0), ((0, 0), (0, 9)))
    given = dict(first=first, cot=cot, w1=qkv_one, p1=proj_one, wm=merge_weight, w2=qkv_two, p2=proj_two)
    args = [given[k] for k in LOADS]
    args += [jnp.asarray(TABLE_OF), seen, mask_token[None], table, gain_one[None], gain_two[None]]
    res, tok, q1, q2 = pl.pallas_call(
        functools.partial(body, sizes),
        out_shape=(
            jax.ShapeDtypeStruct((CELLS, 1024), BF),
            jax.ShapeDtypeStruct((576, 512), BF),
            jax.ShapeDtypeStruct((32, 192), F32),
            jax.ShapeDtypeStruct((64, 384), F32),
        ),
        in_specs=[pl.BlockSpec(memory_space=pl.ANY)] * len(LOADS) + [pl.BlockSpec(memory_space=pltpu.VMEM)] * len(SMALL),
        out_specs=[pl.BlockSpec(memory_space=pltpu.VMEM)] * 4,
        scratch_shapes=list(SCRATCH.values()),
        compiler_params=pltpu.CompilerParams(
            collective_id=0, has_side_effects=True, vmem_limit_bytes=62 * 1024 * 1024),
        cost_estimate=pl.CostEstimate(flops=9 * 10 ** 9, bytes_accessed=24 * 10 ** 6, transcendentals=10 ** 6),
    )(*args)
    result = res.reshape(12, 6, 2, 1024).transpose(2, 0, 1, 3)
    grad_tokens = tok.reshape(2, 12, 24, 512).transpose(0, 2, 1, 3)
    return (result, grad_tokens, q1, q2)


def solution(mesh):
    sizes = (mesh.shape["lon"], mesh.shape["lat"])
    split = P(None, "lon", "lat", None)

    def run(*args):
        return shards(*args, sizes)

    return jax.shard_map(
        run,
        mesh=mesh,
        in_specs=(split, P(None, "lon", "lat")) + (P(),) * 10 + (split,),
        out_specs=(split, split, P("lon", "lat"), P("lon", "lat")),
        check_vma=False,
    )
```

time: 618 us -> 110 us (0.18)
  waiting for transfers between devices: 249 us -> 0 us
  local copies, waits for them, and re-layouts: 214 us -> 9.72 us
  Pallas kernels: 0 us -> 97.6 us
  matrix products: 65.5 us -> 0 us
  other arithmetic: 42.4 us -> 1.44 us
  starting transfers between devices: 27.8 us -> 0 us
  between operations: 15.1 us -> 0.64 us
    reduce_scatter x2 -> x0, waiting for transfers between devices: 141 us -> none  [reduce_weight(): lax.psum_scatter(term.astype(jnp.bfloat16), 'lon', scatter_dimension=0, t...]
    gather x4 -> x0, local copies, waits for them, and re-layouts: 101 us -> none  [window_core(): score = score + table[:, relative_index()][None]]
    pallas_call x0 -> x1, Pallas kernels: none -> 97.6 us  [shards(): pl.pallas_call(functools.partial(body, sizes), out_shape=(jax.ShapeDtypeS...]
    unnamed x6 -> x0, waiting for transfers between devices: 71.4 us -> none
    dot_general x24 -> x0, matrix products: 65.5 us -> none  [the longest x6 12.7 us: window_core(): jnp.einsum('bhnm,bmhd->bnhd', weights, value, preferred_element_type=jnp....]
    ppermute x16 -> x0, waiting for transfers between devices: 37 us -> none  [shifted(): return lax.ppermute(block, axis, route)]
    unnamed x121 -> x3, local copies, waits for them, and re-layouts: 32.4 us -> 4.83 us
    ppermute x16 -> x0, starting transfers between devices: 27.4 us -> none  [shifted(): return lax.ppermute(block, axis, route)]
  transfers between devices with their start and end apart: 20 -> 0, of which waited for: 15 -> 0; matrix products, arithmetic and copies ran while one was open for 26% -> 0% of each run, Pallas kernels for 0% -> 0%
where the time goes in v1:
time: 110 us; the launch traced here: 109 us
  Pallas kernels  97.6 us (89%)
  local copies, waits for them, and re-layouts  9.72 us (9%)
  other arithmetic  1.44 us (1%)
    pallas_call x1, Pallas kernels, shards(): pl.pallas_call(functools.partial(body, sizes), out_shape=(jax.ShapeDtypeS...  97.6 us
    unnamed x3, local copies, waits for them, and re-layouts  4.83 us

profile of v1, /device:TPU:0, one launch (start us, length us, event | category | flops | bytes accessed | tf_op | source)
XLA Modules:
  0.0 109.4 jit_solution(5482467187301331150)
XLA Ops:
  0.6 0.7 copy.19
  1.3 0.6 reshape.25.refs_8_
  1.9 1.4 %select_maximum_fusion.refs_10_ = f32[24,768]{1,0:T(8,128)} fusion(f32[16,759]{1,0:T(8,128)} %param.24, f32[8,759]{1,0:T(8,128)} %param.19), kind=kLoop, calls=%fused_computation | loop fusion | flops 73728 | bytes 146592 | tf_op jit(solution)/shard_map/concatenate | solution.py:618
  3.4 1.8 %reshape.24.refs_1_ = bf16[144,1024]{1,0:T(8,128)(2,1)} reshape(bf16[12,6,2,1024]{3,2,1,0:T(2,128)(2,1)} %bitcast.13) | data formatting | bytes 589824 | tf_op jit(solution)/shard_map/reshape | solution.py:616
  5.2 97.6 %shard_map.165 = (bf16[144,1024]{1,0:T(8,128)(2,1)}, bf16[576,512]{1,0:T(8,128)(2,1)}, f32[32,192]{1,0:T(8,128)}, f32[64,384]{1,0:T(8,128)}) custom-call(bf16[576,512]{1,0:T(8,128)(2,1)} %bitcast.16, bf16[144,1024]{1,0:T(8,128)(2,1)} %reshape.24.refs_1_, bf16[512,1536]{1,0:T(8,128)(2,1)} %refs_2_.1, bf16[512,512]{1,0:T(8,128)(2,1)} %refs_3_.1, ...), custom_call_target="tpu_custom_call" | custom-call | flops 8999999488 | bytes 24000000 | tf_op jit(solution)/shard_map/pallas_call | solution.py:622
  102.8 1.8 %reshape.26 = bf16[12,6,2,1024]{3,2,1,0:T(2,128)(2,1)} reshape(bf16[144,1024]{1,0:T(8,128)(2,1)} %get-tuple-element.8) | data formatting | bytes 589824 | tf_op jit(solution)/shard_map/reshape | solution.py:637
  104.6 1.9 %copy.23 = bf16[2,24,12,512]{3,1,2,0:T(8,128)(2,1)} copy(bf16[2,24,12,512]{3,1,2,0:T(8,128)(2,1)} %bitcast.12) | data formatting | bytes 1179648
  106.5 1.4 %copy.24 = f32[32,192]{1,0:T(8,128)} copy(f32[32,192]{1,0:T(8,128)} %get-tuple-element.18) | data formatting | bytes 49152
  107.9 1.5 %copy.25 = f32[64,384]{1,0:T(8,128)} copy(f32[64,384]{1,0:T(8,128)} %get-tuple-element.19) | data formatting | bytes 196608

commit v2 on v1

--- a/solution.py
+++ b/solution.py
@@ -88,7 +88,7 @@
     for x in range(3):
         for y in range(23):
             for z in range(11):
-                flip[((2 - x) * 23 + 22 - y) * 11 + 10 - z] = z * 69 + x * 23 + y
+                flip[(x * 23 + y) * 11 + z] = z * 69 + x * 23 + y
     pick = [-1] * 768
     for z in range(11):
         for v in range(2):
@@ -103,7 +103,7 @@
 for _n, _rows in enumerate(INDEX.values()):
     TABLE_OF[:len(_rows), _n] = _rows
 
-SHAPES = dict(first=(576, 512), cot=(CELLS, 1024), w1=(512, 1536), p1=(512, 512), p2=(1024, 1024),
+SHAPES = dict(first=(576, 512), cot=(72, 2, 1024), w1=(512, 1536), p1=(512, 512), p2=(1024, 1024),
               wm=(2048, 1024), w2=(1024, 3072))
 LOADS = tuple(SHAPES)
 
@@ -133,10 +133,13 @@
 
 SCRATCH = dict(
     {k: pltpu.VMEM(SHAPES[k], BF) for k in LOADS},
-    parts=pltpu.VMEM((72, 768), F32),
+    mats=pltpu.VMEM((608, 576), BF),
+    matr=pltpu.VMEM((576, 608), BF),
+    tables=pltpu.VMEM((24, 768), F32),
+    shifted=pltpu.VMEM((1152, 768), F32),
     ext=pltpu.VMEM((24, 24, 264), F32),
-    bias=pltpu.VMEM((24, CELLS, CELLS), F32),
-    madd=pltpu.VMEM((2, CELLS, CELLS), F32),
+    bias=pltpu.VMEM((12, CELLS, 288), F32),
+    madd=pltpu.VMEM((CELLS, 288), F32),
     xr=pltpu.VMEM((4, 608, 512), BF),
     xs=pltpu.VMEM((4, 272, 512), BF),
     cr=pltpu.VMEM((2, 192, 1024), BF),
@@ -146,7 +149,7 @@
     rolled1t=pltpu.VMEM((512, 576), BF),
     qkv1=pltpu.VMEM((576, 1536), BF),
     dqkv1=pltpu.VMEM((576, 1536), BF),
-    prob1=pltpu.VMEM((16, 288, CELLS), BF),
+    prob1=pltpu.VMEM((16, CELLS, 288), BF),
     mixed1=pltpu.VMEM((576, 512), BF),
     out1=pltpu.VMEM((576, 512), BF),
     gm1=pltpu.VMEM((576, 512), BF),
@@ -159,12 +162,16 @@
     half2=pltpu.VMEM((2, CELLS, 512), BF),
     theirs2=pltpu.VMEM((CELLS, 512), BF),
     halft=pltpu.VMEM((2, 512, CELLS), BF),
-    prob2=pltpu.VMEM((8, 288, CELLS), BF),
     mixed2=pltpu.VMEM((CELLS, 1024), BF),
     ct=pltpu.VMEM((CELLS, 1024), BF),
     gm2=pltpu.VMEM((CELLS, 1024), BF),
     res=pltpu.VMEM((CELLS, 1024), BF),
     gs=pltpu.VMEM((CELLS, 1024), BF),
+    v_res=pltpu.VMEM((72, 2, 1024), BF),
+    v_tok=pltpu.VMEM((576, 512), BF),
+    v_q1=pltpu.VMEM((32, 192), F32),
+    v_q2=pltpu.VMEM((64, 384), F32),
+    out_sem=pltpu.SemaphoreType.DMA((4,)),
     b2=pltpu.VMEM((3, 64, 64, 128), BF),
     b2r0=pltpu.VMEM((3, 3, 16, 64, 128), BF),
     b2r1=pltpu.VMEM((3, 3, 4, 64, 128), BF),
@@ -182,7 +189,7 @@
     core_send=pltpu.SemaphoreType.DMA((3,)),
     core_recv=pltpu.SemaphoreType.DMA((3,)),
 )
-SMALL = ("index", "seen", "mask", "table", "gain1", "gain2")
+SMALL = ("index", "seen", "mask", "table1", "table2", "gain1", "gain2")
 OUTPUTS = ("o_res", "o_tok", "o_q1", "o_q2")
 
 ORDERS = (("z", "x", "y"), ("x", "y", "z"), ("y", "z", "x"))
@@ -227,7 +234,6 @@
             partners.append(along(axis, k))
     for who in partners:
         pl.semaphore_signal(barrier, inc=1, device_id=who, device_id_type=MESH)
-    pl.semaphore_wait(barrier, len(partners))
 
     def exchange(n, segs, source, target, to):
         copies = []
@@ -255,51 +261,76 @@
         hit = col == lax.broadcasted_iota(jnp.int32, (size, columns), 1)
         return jnp.where(hit, 1.0, 0.0).astype(BF)
 
+    def put(n, name):
+        copy = pltpu.make_async_copy(getattr(R, "v_" + name), getattr(R, "o_" + name), R.out_sem.at[n])
+        copy.start()
+        return copy
+
+    seen = R.in_seen[...]
+    seen = jnp.concatenate([seen[:, 0, :], seen[:, 1, :]], axis=0).astype(F32).astype(BF)
     row = lax.broadcasted_iota(jnp.int32, (576, 24), 0)
     col = lax.broadcasted_iota(jnp.int32, (576, 24), 1)
-    per = nn(jnp.where(row // 24 == col, 1.0, 0.0).astype(BF), R.in_seen[...].astype(F32).astype(BF))
+    per = nn(jnp.where(row // 24 == col, 1.0, 0.0).astype(BF), seen)
     present = jnp.sum(jnp.where(lax.rem(row, 24) == col, per, 0.0), axis=-1, keepdims=True) > 0.5
 
+    R.mats[...] = take("s1", 0, 608, 576)
     loads.first.wait()
     R.first[...] = jnp.where(present, R.first[...].astype(F32), R.in_mask[...].astype(BF).astype(F32)).astype(BF)
-    R.xs[0] = nn(take("s1", 336, 272, 576), R.first[...]).astype(BF)
+    R.xs[0] = nn(R.mats[336:, :], R.first[...]).astype(BF)
+    pl.semaphore_wait(barrier, len(partners))
     halo0 = exchange(0, SEG1, R.xs.at[0], R.xr.at[0], behind)
-    R.xr[0, 0:336] = nn(take("s1", 0, 336, 576), R.first[...]).astype(BF)
+    R.xr[0, 0:336] = nn(R.mats[0:336, :], R.first[...]).astype(BF)
     loads.cot.wait()
-    R.cs[0] = nn(take("sc", 48, 144, CELLS), R.cot[...]).astype(BF)
+    cot = R.cot[...].reshape(CELLS, 1024)
+    R.cs[0] = nn(take("sc", 48, 144, CELLS), cot).astype(BF)
     halo_c = exchange(4, SEG2, R.cs.at[0], R.cr.at[0], behind)
-    R.cr[0, 0:48] = nn(take("sc", 0, 48, CELLS), R.cot[...]).astype(BF)
-
-    table = R.in_table[...]
+    R.cr[0, 0:48] = nn(take("sc", 0, 48, CELLS), cot).astype(BF)
+    R.matr[...] = take("r1", 0, 576, 608)
+    R.mats[...] = take("s2", 0, 608, 576)
+
+    R.tables[...] = jnp.zeros((24, 768), F32)
+    R.tables[0:8, 0:759] = R.in_table1[...]
+    R.tables[8:24, 0:759] = R.in_table2[...]
+    table = R.tables[...]
     high = table.astype(BF).astype(F32)
     mid = (table - high).astype(BF).astype(F32)
     low = table - high - mid
     parts = jnp.concatenate([high, mid, low], axis=0).astype(BF)
-    R.parts[...] = nn(parts, take("flip", 0, 768, 768))
+    parts = nn(parts, take("flip", 0, 768, 768))
     picked = take("pick", 0, 768, 264)
-    for v in range(2):
-        for l in range(12):
-            shift = (1 - v) * 23 + 11 - l
-            moved = pltpu.roll(R.parts[...], (768 - shift) % 768, 1) if shift else R.parts[...]
-            got = nn(moved.astype(BF), picked)
-            R.ext[:, v * 12 + l, :] = got[0:24] + got[24:48] + got[48:72]
+
+    def extend(first, heads):
+        part = jnp.concatenate([parts[24 * k + first:24 * k + first + heads] for k in range(3)], axis=0)
+        for v in range(2):
+            for l in range(12):
+                shift = (1 - v) * 23 + 11 - l
+                moved = pltpu.roll(part, (768 - shift) % 768, 1) if shift else part
+                at = (v * 12 + l) * 3 * heads
+                R.shifted[at:at + 3 * heads] = moved
+        got = nn(R.shifted[0:72 * heads].astype(BF), picked)
+        for n in range(24):
+            at = n * 3 * heads
+            R.ext[first:first + heads, n, :] = (
+                got[at:at + heads] + got[at + heads:at + 2 * heads] + got[at + 2 * heads:at + 3 * heads])
+
+    extend(0, 8)
     rows = lax.broadcasted_iota(jnp.int32, (CELLS, CELLS), 0)
     cols = lax.broadcasted_iota(jnp.int32, (CELLS, CELLS), 1)
-    apart = jnp.logical_xor(rows < HALF, cols < HALF)
-    apart_add = jnp.where(apart, NEG, 0.0).astype(F32) * jnp.where(last, 1.0, 0.0).astype(F32)
-    R.madd[0] = jnp.zeros((CELLS, CELLS), F32)
-    R.madd[1] = apart_add
-
-    def expand(h):
+    apart = jnp.where(jnp.logical_xor(rows < HALF, cols < HALF), NEG, 0.0).astype(F32)
+    apart = apart * jnp.where(last, 1.0, 0.0).astype(F32)
+    R.madd[...] = jnp.concatenate([apart, apart], axis=1)
+
+    def expand(pair):
+        one, two = R.ext[2 * pair], R.ext[2 * pair + 1]
         for a in range(6):
-            piece = R.ext[h, :, (5 - a) * 24:(5 - a) * 24 + CELLS]
-            R.bias[h, a * 24:(a + 1) * 24, :] = piece
-
-    def expand_masked(h):
-        expand(8 + h)
-        R.bias[8 + h] = R.bias[8 + h] + R.madd[1]
-
-    loop(8, expand)
+            at = slice((5 - a) * 24, (5 - a) * 24 + CELLS)
+            R.bias[pair, a * 24:(a + 1) * 24, :] = jnp.concatenate([one[:, at], two[:, at]], axis=1)
+
+    def expand_masked(pair):
+        expand(4 + pair)
+        R.bias[4 + pair] = R.bias[4 + pair] + R.madd[...]
+
+    loop(4, expand)
 
     lane = lax.broadcasted_iota(jnp.int32, (1, 128), 1)
     left = jnp.where(lane < 64, 1.0, 0.0).astype(BF)
@@ -309,40 +340,34 @@
     def stack(t):
         return jnp.concatenate([t * left, t * right], axis=0)
 
-    def attend(qkv, prob, mixed, unit, rows, pair, width, bias):
-        at = lambda part: pl.ds(pl.multiple_of(part * width + pair * 128, 128), 128)
-        q = qkv[rows, at(0)] * BF(0.125)
-        k = qkv[rows, at(1)]
-        v = qkv[rows, at(2)]
-        score = nt(stack(q), k) + bias
-        top = jnp.max(score, axis=-1, keepdims=True)
-        expo = jnp.exp(score - top)
-        p = (expo * (1.0 / jnp.sum(expo, axis=-1, keepdims=True))).astype(BF)
-        prob[unit] = p
-        o = nn(p, v)
-        mixed[rows, at(0)] = jnp.where(is_left, o[:CELLS], o[CELLS:]).astype(BF)
-
-    def attend_back(qkv, prob, grad, out, unit, rows, pair, width):
-        at = lambda part: pl.ds(pl.multiple_of(part * width + pair * 128, 128), 128)
-        q = qkv[rows, at(0)] * BF(0.125)
-        k = qkv[rows, at(1)]
-        v = qkv[rows, at(2)]
-        go = stack(grad[rows, at(0)])
-        pb = prob[unit]
-        p = pb.astype(F32)
-        gw = nt(go, v)
-        gs = (p * (gw - jnp.sum(p * gw, axis=-1, keepdims=True))).astype(BF)
-        gq = nn(gs, k)
-        out[rows, at(0)] = (jnp.where(is_left, gq[:CELLS], gq[CELLS:]) * 0.125).astype(BF)
-        out[rows, at(1)] = tn(gs, stack(q)).astype(BF)
-        out[rows, at(2)] = tn(pb, go).astype(BF)
-
+    def at(part, pair, width):
+        return pl.ds(pl.multiple_of(part * width + pair * 128, 128), 128)
+
+    def heads_of(t):
+        return jnp.where(is_left, t[:CELLS], t[CELLS:])
+
+    def attend(q2, k, v, bias):
+        score = [nt(b, a) + c for a, b, c in zip(q2, k, bias)]
+        expo = [jnp.exp(t - jnp.max(t, axis=0, keepdims=True)) for t in score]
+        p = [t * (1.0 / jnp.sum(t, axis=0, keepdims=True)) for t in expo]
+        pb = [t.astype(BF) for t in p]
+        o = [heads_of(tn(a, b)).astype(BF) for a, b in zip(pb, v)]
+        return p, pb, o
+
+    def attend_back(q2, k, v, p, pb, go):
+        gw = [nt(a, b) for a, b in zip(v, go)]
+        gs = [(a * (b - jnp.sum(a * b, axis=0, keepdims=True))).astype(BF) for a, b in zip(p, gw)]
+        gv = [nn(a, b).astype(BF) for a, b in zip(pb, go)]
+        gk = [nn(a, b).astype(BF) for a, b in zip(gs, q2)]
+        gq = [(heads_of(tn(a, b)) * 0.125).astype(BF) for a, b in zip(gs, k)]
+        return gq, gk, gv
+
+    gain1 = R.in_gain1[...]
     wait(halo0)
-    gain1 = R.in_gain1[...]
 
     def norm1(w):
         rows = pl.ds(pl.multiple_of(w * CELLS, 16), CELLS)
-        t = nn(take("r1", pl.multiple_of(w * CELLS, 16), CELLS, 608), R.xr[0])
+        t = nn(R.matr[rows, :], R.xr[0])
         R.x1[rows, :] = t.astype(BF)
         dev, inv = norm_stats(t)
         R.rolled1[rows, :] = (dev * inv * gain1).astype(BF)
@@ -356,13 +381,22 @@
 
     loop(6, qkv1)
 
+    def two_windows(u):
+        pair, half = u // 2, lax.rem(u, 2)
+        return pair, [pl.ds(pl.multiple_of((half * 2 + k) * CELLS, 16), CELLS) for k in range(2)]
+
     def fwd1(u):
-        pair, w = u // 4, lax.rem(u, 4)
-        rows = pl.ds(pl.multiple_of(w * CELLS, 16), CELLS)
-        bias = R.bias[pl.ds(pair * 2, 2)] + R.madd[lax.rem(w, 2)][None]
-        attend(R.qkv1, R.prob1, R.mixed1, u, rows, pair, 512, bias.reshape(288, CELLS))
-
-    loop(16, fwd1)
+        pair, rows = two_windows(u)
+        q2 = [stack(R.qkv1[r, at(0, pair, 512)] * BF(0.125)) for r in rows]
+        k = [R.qkv1[r, at(1, pair, 512)] for r in rows]
+        v = [R.qkv1[r, at(2, pair, 512)] for r in rows]
+        bias = R.bias[pair]
+        _, pb, o = attend(q2, k, v, [bias, bias + R.madd[...]])
+        for n in range(2):
+            R.prob1[u * 2 + n] = pb[n]
+            R.mixed1[rows[n], at(0, pair, 512)] = o[n]
+
+    loop(8, fwd1)
     loads.p1.wait()
 
     def proj1(w):
@@ -372,10 +406,13 @@
 
     loop(4, proj1)
 
-    R.xs[1] = nn(take("s2", 336, 272, 576), R.out1[...]).astype(BF)
+    R.xs[1] = nn(R.mats[336:, :], R.out1[...]).astype(BF)
     halo1 = exchange(1, SEG1, R.xs.at[1], R.xr.at[1], behind)
-    R.xr[1, 0:336] = nn(take("s2", 0, 336, 576), R.out1[...]).astype(BF)
-    loop(16, expand_masked)
+    R.xr[1, 0:336] = nn(R.mats[0:336, :], R.out1[...]).astype(BF)
+    extend(8, 16)
+    loop(8, expand_masked)
+    R.mats[...] = take("s3", 0, 608, 576)
+    R.matr[...] = take("r2", 0, 576, 608)
     wait(halo_c)
     R.ct[...] = nn(take("rc", 0, CELLS, 192), R.cr[0]).astype(BF)
     loads.p2.wait()
@@ -387,7 +424,7 @@
     loop(4, grad_mixed2)
     R.rolled1t[...] = R.rolled1[...].T
     wait(halo1)
-    R.merged[...] = nn(take("r2", 0, 576, 608), R.xr[1]).astype(BF)
+    R.merged[...] = nn(R.matr[...], R.xr[1]).astype(BF)
     loads.wm.wait()
     acc = nn(R.merged[0:CELLS, :], R.wm[0:512, :])
     for s in range(1, 4):
@@ -418,14 +455,20 @@
         recv_sem=R.core_recv.at[0], device_id=other, device_id_type=MESH)
     core0.start()
 
-    everyrow = pl.ds(0, CELLS)
-
-    def fwd2(u):
-        bias = R.bias[pl.ds(8 + u * 2, 2)].reshape(288, CELLS)
-        attend(R.qkv2, R.prob2, R.mixed2, u, everyrow, u, 1024, bias)
-        attend_back(R.qkv2, R.prob2, R.gm2, R.dqkv2.at[0], u, everyrow, u, 1024)
-
-    loop(8, fwd2)
+    def both2(u):
+        pairs = (u * 2, u * 2 + 1)
+        q2 = [stack(R.qkv2[:, at(0, c, 1024)] * BF(0.125)) for c in pairs]
+        k = [R.qkv2[:, at(1, c, 1024)] for c in pairs]
+        v = [R.qkv2[:, at(2, c, 1024)] for c in pairs]
+        go = [stack(R.gm2[:, at(0, c, 1024)]) for c in pairs]
+        p, pb, o = attend(q2, k, v, [R.bias[4 + c] for c in pairs])
+        back = attend_back(q2, k, v, p, pb, go)
+        for n, c in enumerate(pairs):
+            R.mixed2[:, at(0, c, 1024)] = o[n]
+            for part in range(3):
+                R.dqkv2[0, :, at(part, c, 1024)] = back[part][n]
+
+    loop(4, both2)
     core1 = pltpu.make_async_remote_copy(
         src_ref=R.dqkv2.at[0], dst_ref=R.dqkv2.at[1], send_sem=R.core_send.at[1],
         recv_sem=R.core_recv.at[1], device_id=other, device_id_type=MESH)
@@ -446,9 +489,12 @@
     R.gs[...] = norm_back(grad_rolled, R.second[...], gain2, R.ct[...])
     for s in range(4):
         R.merged[s * CELLS:(s + 1) * CELLS, :] = nt(R.gs[...], R.wm[s * 512:(s + 1) * 512, :]).astype(BF)
-    R.xs[2] = nn(take("s3", 336, 272, 576), R.merged[...]).astype(BF)
+    R.xs[2] = nn(R.mats[336:, :], R.merged[...]).astype(BF)
     halo2 = exchange(2, SEG1, R.xs.at[2], R.xr.at[2], ahead)
-    R.xr[2, 0:336] = nn(take("s3", 0, 336, 576), R.merged[...]).astype(BF)
+    R.xr[2, 0:336] = nn(R.mats[0:336, :], R.merged[...]).astype(BF)
+
+    R.mats[...] = take("s4", 0, 608, 576)
+    R.matr[...] = take("r3", 0, 576, 608)
 
     branch = nn(R.mixed2[...], R.p2[...]).astype(BF).astype(F32)
     R.res[...] = (R.second[...].astype(F32) + branch).astype(BF)
@@ -522,7 +568,7 @@
     big = rs_start(R.b2, R.b2r0, 0, 0)
 
     wait(halo2)
-    R.g1[...] = nn(take("r3", 0, 576, 608), R.xr[2]).astype(BF)
+    R.g1[...] = nn(R.matr[...], R.xr[2]).astype(BF)
 
     def grad_mixed1(w):
         rows = pl.ds(pl.multiple_of(w * CELLS, 16), CELLS)
@@ -531,11 +577,18 @@
     loop(4, grad_mixed1)
 
     def bwd1(u):
-        pair, w = u // 4, lax.rem(u, 4)
-        rows = pl.ds(pl.multiple_of(w * CELLS, 16), CELLS)
-        attend_back(R.qkv1, R.prob1, R.gm1, R.dqkv1, u, rows, pair, 512)
-
-    loop(16, bwd1)
+        pair, rows = two_windows(u)
+        q2 = [stack(R.qkv1[r, at(0, pair, 512)] * BF(0.125)) for r in rows]
+        k = [R.qkv1[r, at(1, pair, 512)] for r in rows]
+        v = [R.qkv1[r, at(2, pair, 512)] for r in rows]
+        go = [stack(R.gm1[r, at(0, pair, 512)]) for r in rows]
+        pb = [R.prob1[u * 2 + n] for n in range(2)]
+        back = attend_back(q2, k, v, [t.astype(F32) for t in pb], pb, go)
+        for n in range(2):
+            for part in range(3):
+                R.dqkv1[rows[n], at(part, pair, 512)] = back[part][n]
+
+    loop(8, bwd1)
 
     def term1(t):
         c = pl.ds(pl.multiple_of(t * 384, 128), 384)
@@ -580,23 +633,27 @@
         R.out1[rows, :] = norm_back(grad, R.x1[rows, :], gain1, R.g1[rows, :])
 
     loop(4, tail1)
-    R.xs[3] = nn(take("s4", 336, 272, 576), R.out1[...]).astype(BF)
+    R.xs[3] = nn(R.mats[336:, :], R.out1[...]).astype(BF)
     halo3 = exchange(3, SEG1, R.xs.at[3], R.xr.at[3], ahead)
-    R.xr[3, 0:336] = nn(take("s4", 0, 336, 576), R.out1[...]).astype(BF)
-
+    R.xr[3, 0:336] = nn(R.mats[0:336, :], R.out1[...]).astype(BF)
+
+    R.matr[...] = take("r4", 0, 576, 608)
     rs_add(mine, R.b1r0, 0, small)
     small = rs_start(mine, R.b1r1, 27, 1)
     rs_add(R.b2, R.b2r1, 1, big)
     big = rs_start(R.b2, R.b2r2, 0, 2)
     wait(halo_r)
-    R.o_res[...] = nn(take("rr", 0, CELLS, 192), R.cr[1]).astype(BF)
+    R.v_res[...] = nn(take("rr", 0, CELLS, 192), R.cr[1]).astype(BF).reshape(72, 2, 1024)
+    puts = [put(0, "res")]
     rs_add(mine, R.b1r1, 1, small)
     small = rs_start(mine, R.b1r2, 27, 2)
     wait(halo3)
-    R.o_tok[...] = jnp.where(present, nn(take("r4", 0, 576, 608), R.xr[3]), 0.0).astype(BF)
+    R.v_tok[...] = jnp.where(present, nn(R.matr[...], R.xr[3]), 0.0).astype(BF)
+    puts.append(put(1, "tok"))
     wait(big)
     for p in range(3):
-        R.o_q2[:, p * 128:(p + 1) * 128] = rs_last(R.b2, R.b2r2, p, big)
+        R.v_q2[:, p * 128:(p + 1) * 128] = rs_last(R.b2, R.b2r2, p, big)
+    puts.append(put(3, "q2"))
     wait(small)
     a, b, m = [rs_last(mine, R.b1r2, p, small) for p in range(3)]
     turned = pltpu.roll(m, 64, 1)
@@ -604,36 +661,53 @@
     a_turned = pltpu.roll(a, 64, 1)
     b_turned = pltpu.roll(b, 64, 1)
     pick = is_left[0:16]
-    R.o_q1[0:16, 0:128] = jnp.where(even, a, jnp.where(pick, turned, a_turned))
-    R.o_q1[16:32, 0:128] = jnp.where(even, b, jnp.where(pick, m, b_turned))
-    R.o_q1[0:16, 128:192] = jnp.where(even, m, a_turned)[:, 0:64]
-    R.o_q1[16:32, 128:192] = jnp.where(even, turned, b_turned)[:, 0:64]
+    R.v_q1[0:16, 0:128] = jnp.where(even, a, jnp.where(pick, turned, a_turned))
+    R.v_q1[16:32, 0:128] = jnp.where(even, b, jnp.where(pick, m, b_turned))
+    R.v_q1[0:16, 128:192] = jnp.where(even, m, a_turned)[:, 0:64]
+    R.v_q1[16:32, 128:192] = jnp.where(even, turned, b_turned)[:, 0:64]
+    puts.append(put(2, "q1"))
+    wait(puts)
+
+
+def hand_on(*refs):
+    copies = [pltpu.make_async_copy(refs[n], refs[4 + n], refs[8].at[n]) for n in range(4)]
+    for c in copies:
+        c.start()
+    for c in copies:
+        c.wait()
 
 
 def shards(tokens, observed, mask_token, gain_one, qkv_one, table_one, proj_one, merge_weight, gain_two, qkv_two,
            table_two, proj_two, cotangent, sizes):
     first = tokens.transpose(0, 2, 1, 3).reshape(576, 512)
-    cot = cotangent.transpose(1, 2, 0, 3).reshape(CELLS, 1024)
-    seen = observed.transpose(0, 2, 1).reshape(24, 24)
-    table = jnp.pad(jnp.concatenate([table_one, table_two], axis=0), ((0, 0), (0, 9)))
+    cot = cotangent.transpose(1, 2, 0, 3).reshape(72, 2, 1024)
+    seen = observed.transpose(2, 0, 1)
     given = dict(first=first, cot=cot, w1=qkv_one, p1=proj_one, wm=merge_weight, w2=qkv_two, p2=proj_two)
     args = [given[k] for k in LOADS]
-    args += [jnp.asarray(TABLE_OF), seen, mask_token[None], table, gain_one[None], gain_two[None]]
-    res, tok, q1, q2 = pl.pallas_call(
+    args += [jnp.asarray(TABLE_OF), seen, mask_token[None], table_one, table_two, gain_one[None], gain_two[None]]
+    shapes = (
+        jax.ShapeDtypeStruct((72, 2, 1024), BF),
+        jax.ShapeDtypeStruct((576, 512), BF),
+        jax.ShapeDtypeStruct((32, 192), F32),
+        jax.ShapeDtypeStruct((64, 384), F32),
+    )
+    outs = pl.pallas_call(
         functools.partial(body, sizes),
-        out_shape=(
-            jax.ShapeDtypeStruct((CELLS, 1024), BF),
-            jax.ShapeDtypeStruct((576, 512), BF),
-            jax.ShapeDtypeStruct((32, 192), F32),
-            jax.ShapeDtypeStruct((64, 384), F32),
-        ),
+        out_shape=shapes,
         in_specs=[pl.BlockSpec(memory_space=pl.ANY)] * len(LOADS) + [pl.BlockSpec(memory_space=pltpu.VMEM)] * len(SMALL),
-        out_specs=[pl.BlockSpec(memory_space=pltpu.VMEM)] * 4,
+        out_specs=[pl.BlockSpec(memory_space=pl.ANY)] * 4,
         scratch_shapes=list(SCRATCH.values()),
         compiler_params=pltpu.CompilerParams(
             collective_id=0, has_side_effects=True, vmem_limit_bytes=62 * 1024 * 1024),
         cost_estimate=pl.CostEstimate(flops=9 * 10 ** 9, bytes_accessed=24 * 10 ** 6, transcendentals=10 ** 6),
     )(*args)
+    res, tok, q1, q2 = pl.pallas_call(
+        hand_on,
+        out_shape=shapes,
+        in_specs=[pl.BlockSpec(memory_space=pl.ANY)] * 4,
+        out_specs=[pl.BlockSpec(memory_space=pl.ANY)] * 4,
+        scratch_shapes=[pltpu.SemaphoreType.DMA((4,))],
+    )(*outs)
     result = res.reshape(12, 6, 2, 1024).transpose(2, 0, 1, 3)
     grad_tokens = tok.reshape(2, 12, 24, 512).transpose(0, 2, 1, 3)
     return (result, grad_tokens, q1, q2)

time: 110 us -> 121 us (1.10)
  Pallas kernels: 97.6 us -> 120 us
  local copies, waits for them, and re-layouts: 9.72 us -> 0 us
  other arithmetic: 1.44 us -> 0 us
    pallas_call x1 -> x2, Pallas kernels: 97.6 us -> 120 us  [the longest x1 87.8 us: shards(): pl.pallas_call(functools.partial(body, sizes), out_shape=shapes, in_specs...]
    unnamed x3 -> x0, local copies, waits for them, and re-layouts: 4.83 us -> none
    reshape x3 -> x0, local copies, waits for them, and re-layouts: 4.17 us -> none  [the longest x1 1.79 us: shards(): result = res.reshape(12, 6, 2, 1024).transpose(2, 0, 1, 3)]
    concatenate x1 -> x0, other arithmetic: 1.44 us -> none  [shards(): jnp.concatenate([table_one, table_two], axis=0)]
where the time goes in v2:
time: 121 us; the launch traced here: 120 us
  Pallas kernels  120 us (99%)
    pallas_call x1, Pallas kernels, shards(): pl.pallas_call(functools.partial(body, sizes), out_shape=shapes, in_specs...  87.8 us
    pallas_call x1, Pallas kernels, shards(): pl.pallas_call(hand_on, out_shape=shapes, in_specs=[pl.BlockSpec(memory_s...  31.9 us

profile of v2, /device:TPU:0, one launch (start us, length us, event | category | flops | bytes accessed | tf_op | source)
XLA Modules:
  0.0 120.5 jit_solution(15566382433849798135)
XLA Ops:
  0.6 87.8 %shard_map.165 = (bf16[72,2,1024]{2,1,0:T(2,128)(2,1)}, bf16[576,512]{1,0:T(8,128)(2,1)}, f32[32,192]{1,0:T(8,128)}, f32[64,384]{1,0:T(8,128)}) custom-call(bf16[576,512]{1,0:T(8,128)(2,1)} %bitcast.16, bf16[72,2,1024]{2,1,0:T(2,128)(2,1)} %bitcast.18, bf16[512,1536]{1,0:T(8,128)(2,1)} %refs_2_.1, bf16[512,512]{1,0:T(8,128)(2,1)} %refs_3_.1, ...), custom_call_target="tpu_custom_call" | custom-call | flops 8999999488 | bytes 24000000 | tf_op jit(solution)/shard_map/pallas_call | solution.py:694
  88.4 31.9 %shard_map.166 = (bf16[72,2,1024]{2,1,0:T(2,128)(2,1)}, bf16[576,512]{1,0:T(8,128)(2,1)}, f32[32,192]{1,0:T(8,128)}, f32[64,384]{1,0:T(8,128)}) custom-call(bf16[72,2,1024]{2,1,0:T(2,128)(2,1)} %get-tuple-element.12.refs_0_, bf16[576,512]{1,0:T(8,128)(2,1)} %get-tuple-element.13.refs_1_, f32[32,192]{1,0:T(8,128)} %get-tuple-element.14.refs_2_, ...), custom_call_target="tpu_custom_call" | custom-call | tf_op jit(solution)/shard_map/pallas_call | solution.py:704

commit v3 on v2

--- a/solution.py
+++ b/solution.py
@@ -365,13 +365,20 @@
     gain1 = R.in_gain1[...]
     wait(halo0)
 
+    def window(w):
+        return pl.ds(pl.multiple_of(w * CELLS, 16), CELLS)
+
+    def tile(n, size=256):
+        return pl.ds(pl.multiple_of(n * size, size), size)
+
+    def place1(n):
+        R.x1[:, tile(n)] = nn(R.matr[...], R.xr[0, :, tile(n)]).astype(BF)
+
     def norm1(w):
-        rows = pl.ds(pl.multiple_of(w * CELLS, 16), CELLS)
-        t = nn(R.matr[rows, :], R.xr[0])
-        R.x1[rows, :] = t.astype(BF)
-        dev, inv = norm_stats(t)
-        R.rolled1[rows, :] = (dev * inv * gain1).astype(BF)
-
+        dev, inv = norm_stats(R.x1[window(w), :].astype(F32))
+        R.rolled1[window(w), :] = (dev * inv * gain1).astype(BF)
+
+    loop(2, place1)
     loop(4, norm1)
     loads.w1.wait()
 
@@ -381,30 +388,28 @@
 
     loop(6, qkv1)
 
-    def two_windows(u):
-        pair, half = u // 2, lax.rem(u, 2)
-        return pair, [pl.ds(pl.multiple_of((half * 2 + k) * CELLS, 16), CELLS) for k in range(2)]
-
-    def fwd1(u):
-        pair, rows = two_windows(u)
-        q2 = [stack(R.qkv1[r, at(0, pair, 512)] * BF(0.125)) for r in rows]
-        k = [R.qkv1[r, at(1, pair, 512)] for r in rows]
-        v = [R.qkv1[r, at(2, pair, 512)] for r in rows]
+    def four(pair):
+        q2 = [stack(R.qkv1[window(w), at(0, pair, 512)] * BF(0.125)) for w in range(4)]
+        k = [R.qkv1[window(w), at(1, pair, 512)] for w in range(4)]
+        v = [R.qkv1[window(w), at(2, pair, 512)] for w in range(4)]
+        return q2, k, v
+
+    def fwd1(pair):
         bias = R.bias[pair]
-        _, pb, o = attend(q2, k, v, [bias, bias + R.madd[...]])
-        for n in range(2):
-            R.prob1[u * 2 + n] = pb[n]
-            R.mixed1[rows[n], at(0, pair, 512)] = o[n]
-
-    loop(8, fwd1)
+        masked = bias + R.madd[...]
+        _, pb, o = attend(*four(pair), [bias, masked, bias, masked])
+        for w in range(4):
+            R.prob1[pair * 4 + w] = pb[w]
+            R.mixed1[window(w), at(0, pair, 512)] = o[w]
+
+    loop(4, fwd1)
     loads.p1.wait()
 
-    def proj1(w):
-        rows = pl.ds(pl.multiple_of(w * CELLS, 16), CELLS)
-        branch = nn(R.mixed1[rows, :], R.p1[...]).astype(BF).astype(F32)
-        R.out1[rows, :] = (R.x1[rows, :].astype(F32) + branch).astype(BF)
-
-    loop(4, proj1)
+    def proj1(n):
+        branch = nn(R.mixed1[...], R.p1[:, tile(n)]).astype(BF).astype(F32)
+        R.out1[:, tile(n)] = (R.x1[:, tile(n)].astype(F32) + branch).astype(BF)
+
+    loop(2, proj1)
 
     R.xs[1] = nn(R.mats[336:, :], R.out1[...]).astype(BF)
     halo1 = exchange(1, SEG1, R.xs.at[1], R.xr.at[1], behind)
@@ -456,7 +461,7 @@
     core0.start()
 
     def both2(u):
-        pairs = (u * 2, u * 2 + 1)
+        pairs = [u * 4 + n for n in range(4)]
         q2 = [stack(R.qkv2[:, at(0, c, 1024)] * BF(0.125)) for c in pairs]
         k = [R.qkv2[:, at(1, c, 1024)] for c in pairs]
         v = [R.qkv2[:, at(2, c, 1024)] for c in pairs]
@@ -468,7 +473,7 @@
             for part in range(3):
                 R.dqkv2[0, :, at(part, c, 1024)] = back[part][n]
 
-    loop(4, both2)
+    loop(2, both2)
     core1 = pltpu.make_async_remote_copy(
         src_ref=R.dqkv2.at[0], dst_ref=R.dqkv2.at[1], send_sem=R.core_send.at[1],
         recv_sem=R.core_recv.at[1], device_id=other, device_id_type=MESH)
@@ -570,25 +575,21 @@
     wait(halo2)
     R.g1[...] = nn(R.matr[...], R.xr[2]).astype(BF)
 
-    def grad_mixed1(w):
-        rows = pl.ds(pl.multiple_of(w * CELLS, 16), CELLS)
-        R.gm1[rows, :] = nt(R.g1[rows, :], R.p1[...]).astype(BF)
-
-    loop(4, grad_mixed1)
-
-    def bwd1(u):
-        pair, rows = two_windows(u)
-        q2 = [stack(R.qkv1[r, at(0, pair, 512)] * BF(0.125)) for r in rows]
-        k = [R.qkv1[r, at(1, pair, 512)] for r in rows]
-        v = [R.qkv1[r, at(2, pair, 512)] for r in rows]
-        go = [stack(R.gm1[r, at(0, pair, 512)]) for r in rows]
-        pb = [R.prob1[u * 2 + n] for n in range(2)]
+    def grad_mixed1(n):
+        R.gm1[:, tile(n)] = nt(R.g1[...], R.p1[tile(n), :]).astype(BF)
+
+    loop(2, grad_mixed1)
+
+    def bwd1(pair):
+        q2, k, v = four(pair)
+        go = [stack(R.gm1[window(w), at(0, pair, 512)]) for w in range(4)]
+        pb = [R.prob1[pair * 4 + w] for w in range(4)]
         back = attend_back(q2, k, v, [t.astype(F32) for t in pb], pb, go)
-        for n in range(2):
+        for w in range(4):
             for part in range(3):
-                R.dqkv1[rows[n], at(part, pair, 512)] = back[part][n]
-
-    loop(8, bwd1)
+                R.dqkv1[window(w), at(part, pair, 512)] = back[part][w]
+
+    loop(4, bwd1)
 
     def term1(t):
         c = pl.ds(pl.multiple_of(t * 384, 128), 384)
@@ -627,11 +628,14 @@
     loop(64, add_core)
     small = rs_start(mine, R.b1r0, 27, 0)
 
+    def grad_rolled1(n):
+        R.gm1[:, tile(n)] = nt(R.dqkv1[...], R.w1[tile(n), :]).astype(BF)
+
     def tail1(w):
-        rows = pl.ds(pl.multiple_of(w * CELLS, 16), CELLS)
-        grad = nt(R.dqkv1[rows, :], R.w1[...])
-        R.out1[rows, :] = norm_back(grad, R.x1[rows, :], gain1, R.g1[rows, :])
-
+        r = window(w)
+        R.out1[r, :] = norm_back(R.gm1[r, :], R.x1[r, :], gain1, R.g1[r, :])
+
+    loop(2, grad_rolled1)
     loop(4, tail1)
     R.xs[3] = nn(R.mats[336:, :], R.out1[...]).astype(BF)
     halo3 = exchange(3, SEG1, R.xs.at[3], R.xr.at[3], ahead)
@@ -670,10 +674,15 @@
 
 
 def hand_on(*refs):
-    copies = [pltpu.make_async_copy(refs[n], refs[4 + n], refs[8].at[n]) for n in range(4)]
-    for c in copies:
+    given, out, held, sem = refs[0:4], refs[4:8], refs[8:12], refs[12]
+    come = [pltpu.make_async_copy(given[n], held[n], sem.at[n]) for n in range(4)]
+    leave = [pltpu.make_async_copy(held[n], out[n], sem.at[4 + n]) for n in range(4)]
+    for c in come:
         c.start()
-    for c in copies:
+    for n in range(4):
+        come[n].wait()
+        leave[n].start()
+    for c in leave:
         c.wait()
 
 
@@ -706,7 +715,7 @@
         out_shape=shapes,
         in_specs=[pl.BlockSpec(memory_space=pl.ANY)] * 4,
         out_specs=[pl.BlockSpec(memory_space=pl.ANY)] * 4,
-        scratch_shapes=[pltpu.SemaphoreType.DMA((4,))],
+        scratch_shapes=[pltpu.VMEM(s.shape, s.dtype) for s in shapes] + [pltpu.SemaphoreType.DMA((8,))],
     )(*outs)
     result = res.reshape(12, 6, 2, 1024).transpose(2, 0, 1, 3)
     grad_tokens = tok.reshape(2, 12, 24, 512).transpose(0, 2, 1, 3)

time: 121 us -> 87.9 us (0.73)
  Pallas kernels: 120 us -> 87 us
    pallas_call x1, Pallas kernels: 31.9 us -> 2.07 us  [shards(): pl.pallas_call(hand_on, out_shape=shapes, in_specs=[pl.BlockSpec(memory_s...]
    pallas_call x1, Pallas kernels: 87.8 us -> 84.9 us  [shards(): pl.pallas_call(functools.partial(body, sizes), out_shape=shapes, in_specs...]
where the time goes in v3:
time: 87.9 us; the launch traced here: 87.8 us
  Pallas kernels  87 us (99%)
    pallas_call x1, Pallas kernels, shards(): pl.pallas_call(functools.partial(body, sizes), out_shape=shapes, in_specs...  84.9 us
    pallas_call x1, Pallas kernels, shards(): pl.pallas_call(hand_on, out_shape=shapes, in_specs=[pl.BlockSpec(memory_s...  2.07 us

profile of v3, /device:TPU:0, one launch (start us, length us, event | category | flops | bytes accessed | tf_op | source)
XLA Modules:
  0.0 87.8 jit_solution(13782413762308632470)
XLA Ops:
  0.6 84.9 %shard_map.165 = (bf16[72,2,1024]{2,1,0:T(2,128)(2,1)}, bf16[576,512]{1,0:T(8,128)(2,1)}, f32[32,192]{1,0:T(8,128)}, f32[64,384]{1,0:T(8,128)}) custom-call(bf16[576,512]{1,0:T(8,128)(2,1)} %bitcast.16, bf16[72,2,1024]{2,1,0:T(2,128)(2,1)} %bitcast.18, bf16[512,1536]{1,0:T(8,128)(2,1)} %refs_2_.1, bf16[512,512]{1,0:T(8,128)(2,1)} %refs_3_.1, ...), custom_call_target="tpu_custom_call" | custom-call | flops 8999999488 | bytes 24000000 | tf_op jit(solution)/shard_map/pallas_call | solution.py:703
  85.5 2.1 %shard_map.166 = (bf16[72,2,1024]{2,1,0:T(2,128)(2,1)}, bf16[576,512]{1,0:T(8,128)(2,1)}, f32[32,192]{1,0:T(8,128)}, f32[64,384]{1,0:T(8,128)}) custom-call(bf16[72,2,1024]{2,1,0:T(2,128)(2,1)} %get-tuple-element.12.refs_0_, bf16[576,512]{1,0:T(8,128)(2,1)} %get-tuple-element.13.refs_1_, f32[32,192]{1,0:T(8,128)} %get-tuple-element.14.refs_2_, ...), custom_call_target="tpu_custom_call" | custom-call | tf_op jit(solution)/shard_map/pallas_call | solution.py:713

commit v4 on v3

--- a/solution.py
+++ b/solution.py
@@ -176,8 +176,9 @@
     b2r0=pltpu.VMEM((3, 3, 16, 64, 128), BF),
     b2r1=pltpu.VMEM((3, 3, 4, 64, 128), BF),
     b2r2=pltpu.VMEM((3, 3, 1, 64, 128), BF),
-    b1=pltpu.VMEM((2, 3, 64, 16, 128), BF),
-    b1c=pltpu.VMEM((3, 64, 16, 128), BF),
+    b1=pltpu.VMEM((3, 64, 16, 128), BF),
+    b1h=pltpu.VMEM((4, 2, 3, 16, 16, 128), BF),
+    b1c=pltpu.VMEM((4, 3, 16, 16, 128), BF),
     b1r0=pltpu.VMEM((3, 3, 16, 16, 128), BF),
     b1r1=pltpu.VMEM((3, 3, 4, 16, 128), BF),
     b1r2=pltpu.VMEM((3, 3, 1, 16, 128), BF),
@@ -186,8 +187,8 @@
     halo_recv=pltpu.SemaphoreType.DMA((18,)),
     rs_send=pltpu.SemaphoreType.DMA((54,)),
     rs_recv=pltpu.SemaphoreType.DMA((54,)),
-    core_send=pltpu.SemaphoreType.DMA((3,)),
-    core_recv=pltpu.SemaphoreType.DMA((3,)),
+    core_send=pltpu.SemaphoreType.DMA((6,)),
+    core_recv=pltpu.SemaphoreType.DMA((6,)),
 )
 SMALL = ("index", "seen", "mask", "table1", "table2", "gain1", "gain2")
 OUTPUTS = ("o_res", "o_tok", "o_q1", "o_q2")
@@ -277,6 +278,18 @@
     loads.first.wait()
     R.first[...] = jnp.where(present, R.first[...].astype(F32), R.in_mask[...].astype(BF).astype(F32)).astype(BF)
     R.xs[0] = nn(R.mats[336:, :], R.first[...]).astype(BF)
+
+    R.tables[...] = jnp.zeros((24, 768), F32)
+    R.tables[0:8, 0:759] = R.in_table1[...]
+    R.tables[8:24, 0:759] = R.in_table2[...]
+    table = R.tables[...]
+    high = table.astype(BF).astype(F32)
+    mid = (table - high).astype(BF).astype(F32)
+    low = table - high - mid
+    parts = jnp.concatenate([high, mid, low], axis=0).astype(BF)
+    parts = nn(parts, take("flip", 0, 768, 768))
+    picked = take("pick", 0, 768, 264)
+
     pl.semaphore_wait(barrier, len(partners))
     halo0 = exchange(0, SEG1, R.xs.at[0], R.xr.at[0], behind)
     R.xr[0, 0:336] = nn(R.mats[0:336, :], R.first[...]).astype(BF)
@@ -287,17 +300,6 @@
     R.cr[0, 0:48] = nn(take("sc", 0, 48, CELLS), cot).astype(BF)
     R.matr[...] = take("r1", 0, 576, 608)
     R.mats[...] = take("s2", 0, 608, 576)
-
-    R.tables[...] = jnp.zeros((24, 768), F32)
-    R.tables[0:8, 0:759] = R.in_table1[...]
-    R.tables[8:24, 0:759] = R.in_table2[...]
-    table = R.tables[...]
-    high = table.astype(BF).astype(F32)
-    mid = (table - high).astype(BF).astype(F32)
-    low = table - high - mid
-    parts = jnp.concatenate([high, mid, low], axis=0).astype(BF)
-    parts = nn(parts, take("flip", 0, 768, 768))
-    picked = take("pick", 0, 768, 264)
 
     def extend(first, heads):
         part = jnp.concatenate([parts[24 * k + first:24 * k + first + heads] for k in range(3)], axis=0)
@@ -498,34 +500,26 @@
     halo2 = exchange(2, SEG1, R.xs.at[2], R.xr.at[2], ahead)
     R.xr[2, 0:336] = nn(R.mats[0:336, :], R.merged[...]).astype(BF)
 
-    R.mats[...] = take("s4", 0, 608, 576)
-    R.matr[...] = take("r3", 0, 576, 608)
-
-    branch = nn(R.mixed2[...], R.p2[...]).astype(BF).astype(F32)
-    R.res[...] = (R.second[...].astype(F32) + branch).astype(BF)
-    R.cs[1] = nn(take("sr", 48, 144, CELLS), R.res[...]).astype(BF)
-    halo_r = exchange(5, SEG2, R.cs.at[1], R.cr.at[1], ahead)
-    R.cr[1, 0:48] = nn(take("sr", 0, 48, CELLS), R.res[...]).astype(BF)
-
     R.halft[0] = R.half2[core].T
     core0.wait()
     R.halft[1] = R.theirs2[...].T
     core1.wait()
 
-    def term2(t):
-        c = pl.ds(pl.multiple_of(t * 384, 128), 384)
+    def term2(yy):
+        c = tile(yy, 768)
         g = nn(R.halft[0], R.dqkv2[0, :, c]) + nn(R.halft[1], R.dqkv2[1, :, c])
         g = g.astype(BF)
-        yy, xx = t // 2, lax.rem(t, 2)
         for zz in range(4):
             for hh in range(2):
                 r = (zz * 2 + hh) * 64
-                at = dict(z=zz, x=hh * 2 + xx, y=yy)
-                for p, order in enumerate(ORDERS):
-                    block = (at[order[0]] * 4 + at[order[1]]) * 4 + at[order[2]]
-                    R.b2[p, block] = g[r:r + 64, p * 128:(p + 1) * 128]
-
-    loop(8, term2)
+                for xx in range(2):
+                    at = dict(z=zz, x=hh * 2 + xx, y=yy)
+                    for p, order in enumerate(ORDERS):
+                        block = (at[order[0]] * 4 + at[order[1]]) * 4 + at[order[2]]
+                        lanes = xx * 384 + p * 128
+                        R.b2[p, block] = g[r:r + 64, lanes:lanes + 128]
+
+    loop(4, term2)
 
     def rs_start(buf, recv, sem0, step):
         copies = []
@@ -557,12 +551,16 @@
             for s in range(step + 1):
                 base = base + place[order[s]] * (16 >> (2 * s))
 
-            def add(b):
-                t = buf[p, base + b].astype(F32) + recv[p, 0, b].astype(F32)
-                t = t + recv[p, 1, b].astype(F32) + recv[p, 2, b].astype(F32)
-                buf[p, base + b] = t.astype(BF)
-
-            loop(size, add)
+            step_of = min(size, 65536 // (buf.shape[2] * buf.shape[3]))
+
+            def add(n):
+                at = pl.ds(base + n * step_of, step_of)
+                near = pl.ds(n * step_of, step_of)
+                t = buf[p, at].astype(F32) + recv[p, 0, near].astype(F32)
+                t = t + recv[p, 1, near].astype(F32) + recv[p, 2, near].astype(F32)
+                buf[p, at] = t.astype(BF)
+
+            loop(size // step_of, add)
 
     def rs_last(buf, recv, p, copies):
         order = ORDERS[p]
@@ -571,6 +569,8 @@
         return t + recv[p, 1, 0].astype(F32) + recv[p, 2, 0].astype(F32)
 
     big = rs_start(R.b2, R.b2r0, 0, 0)
+    R.mats[...] = take("s4", 0, 608, 576)
+    R.matr[...] = take("r3", 0, 576, 608)
 
     wait(halo2)
     R.g1[...] = nn(R.matr[...], R.xr[2]).astype(BF)
@@ -591,41 +591,42 @@
 
     loop(4, bwd1)
 
+    def to_core(t):
+        return pltpu.make_async_remote_copy(
+            src_ref=R.b1h.at[t, 1 - core], dst_ref=R.b1c.at[t], send_sem=R.core_send.at[2 + t],
+            recv_sem=R.core_recv.at[2 + t], device_id=other, device_id_type=MESH)
+
     def term1(t):
         c = pl.ds(pl.multiple_of(t * 384, 128), 384)
         g = nn(R.rolled1t[...], R.dqkv1[:, c])
+        pick = is_left[0:16]
         for zz in range(4):
             for hh in range(2):
                 for cc in range(2):
                     r = ((zz * 2 + hh) * 2 + cc) * 32
                     upper = g[r:r + 16, 128:256]
                     lower = pltpu.roll(g[r + 16:r + 32, 128:256], 64, 1)
-                    pick = is_left[0:16]
                     mixes = (jnp.where(pick, upper, lower), jnp.where(pick, lower, upper))
                     for odd in range(2):
-                        at = dict(z=zz, x=hh * 2 + odd, y=t)
                         lanes = slice(odd * 256, odd * 256 + 128)
                         pieces = (g[r:r + 16, lanes], g[r + 16:r + 32, lanes], mixes[odd])
-                        for p, order in enumerate(ORDERS):
-                            block = (at[order[0]] * 4 + at[order[1]]) * 4 + at[order[2]]
-                            R.b1[cc, p, block] = pieces[p].astype(BF)
+                        for p in range(3):
+                            R.b1h[t, cc, p, zz * 4 + hh * 2 + odd] = pieces[p].astype(BF)
+        to_core(t).start()
 
     loop(4, term1)
-    core2 = pltpu.make_async_remote_copy(
-        src_ref=R.b1.at[1 - core], dst_ref=R.b1c, send_sem=R.core_send.at[2],
-        recv_sem=R.core_recv.at[2], device_id=other, device_id_type=MESH)
-    core2.start()
     rs_add(R.b2, R.b2r0, 0, big)
     big = rs_start(R.b2, R.b2r1, 0, 1)
 
-    core2.wait()
-    mine = R.b1.at[core]
-
-    def add_core(b):
-        for p in range(3):
-            mine[p, b] = (mine[p, b].astype(F32) + R.b1c[p, b].astype(F32)).astype(BF)
-
-    loop(64, add_core)
+    for t in range(4):
+        to_core(t).wait()
+        for p, order in enumerate(ORDERS):
+            g = R.b1h[t, core, p].astype(F32) + R.b1c[t, p].astype(F32)
+            for n in range(16):
+                at = dict(z=n // 4, x=n % 4, y=t)
+                block = (at[order[0]] * 4 + at[order[1]]) * 4 + at[order[2]]
+                R.b1[p, block] = g[n].astype(BF)
+    mine = R.b1
     small = rs_start(mine, R.b1r0, 27, 0)
 
     def grad_rolled1(n):
@@ -640,6 +641,12 @@
     R.xs[3] = nn(R.mats[336:, :], R.out1[...]).astype(BF)
     halo3 = exchange(3, SEG1, R.xs.at[3], R.xr.at[3], ahead)
     R.xr[3, 0:336] = nn(R.mats[0:336, :], R.out1[...]).astype(BF)
+
+    branch = nn(R.mixed2[...], R.p2[...]).astype(BF).astype(F32)
+    R.res[...] = (R.second[...].astype(F32) + branch).astype(BF)
+    R.cs[1] = nn(take("sr", 48, 144, CELLS), R.res[...]).astype(BF)
+    halo_r = exchange(5, SEG2, R.cs.at[1], R.cr.at[1], ahead)
+    R.cr[1, 0:48] = nn(take("sr", 0, 48, CELLS), R.res[...]).astype(BF)
 
     R.matr[...] = take("r4", 0, 576, 608)
     rs_add(mine, R.b1r0, 0, small)

time: 87.9 us -> 87.5 us (level)
  no operation moved by 1% of the time
where the time goes in v4:
time: 87.5 us; the launch traced here: 87.4 us
  Pallas kernels  86.5 us (99%)
    pallas_call x1, Pallas kernels, shards(): pl.pallas_call(functools.partial(body, sizes), out_shape=shapes, in_specs...  84.5 us
    pallas_call x1, Pallas kernels, shards(): pl.pallas_call(hand_on, out_shape=shapes, in_specs=[pl.BlockSpec(memory_s...  2.07 us

profile of v4, /device:TPU:0, one launch (start us, length us, event | category | flops | bytes accessed | tf_op | source)
XLA Modules:
  0.0 87.4 jit_solution(9797330802642491382)
XLA Ops:
  0.6 84.5 %shard_map.165 = (bf16[72,2,1024]{2,1,0:T(2,128)(2,1)}, bf16[576,512]{1,0:T(8,128)(2,1)}, f32[32,192]{1,0:T(8,128)}, f32[64,384]{1,0:T(8,128)}) custom-call(bf16[576,512]{1,0:T(8,128)(2,1)} %bitcast.16, bf16[72,2,1024]{2,1,0:T(2,128)(2,1)} %bitcast.18, bf16[512,1536]{1,0:T(8,128)(2,1)} %refs_2_.1, bf16[512,512]{1,0:T(8,128)(2,1)} %refs_3_.1, ...), custom_call_target="tpu_custom_call" | custom-call | flops 8999999488 | bytes 24000000 | tf_op jit(solution)/shard_map/pallas_call | solution.py:710
  85.1 2.1 %shard_map.166 = (bf16[72,2,1024]{2,1,0:T(2,128)(2,1)}, bf16[576,512]{1,0:T(8,128)(2,1)}, f32[32,192]{1,0:T(8,128)}, f32[64,384]{1,0:T(8,128)}) custom-call(bf16[72,2,1024]{2,1,0:T(2,128)(2,1)} %get-tuple-element.12.refs_0_, bf16[576,512]{1,0:T(8,128)(2,1)} %get-tuple-element.13.refs_1_, f32[32,192]{1,0:T(8,128)} %get-tuple-element.14.refs_2_, ...), custom_call_target="tpu_custom_call" | custom-call | tf_op jit(solution)/shard_map/pallas_call | solution.py:720

commit v5 on v4

--- a/solution.py
+++ b/solution.py
@@ -173,8 +173,10 @@
     v_q2=pltpu.VMEM((64, 384), F32),
     out_sem=pltpu.SemaphoreType.DMA((4,)),
     b2=pltpu.VMEM((3, 64, 64, 128), BF),
-    b2r0=pltpu.VMEM((3, 3, 16, 64, 128), BF),
-    b2r1=pltpu.VMEM((3, 3, 4, 64, 128), BF),
+    b2v0=pltpu.VMEM((3, 2, 8, 64, 128), BF),
+    b2r0=pltpu.VMEM((3, 2, 16, 64, 128), BF),
+    b2v1=pltpu.VMEM((3, 2, 2, 64, 128), BF),
+    b2r1=pltpu.VMEM((3, 2, 4, 64, 128), BF),
     b2r2=pltpu.VMEM((3, 3, 1, 64, 128), BF),
     b1=pltpu.VMEM((3, 64, 16, 128), BF),
     b1h=pltpu.VMEM((4, 2, 3, 16, 16, 128), BF),
@@ -187,6 +189,8 @@
     halo_recv=pltpu.SemaphoreType.DMA((18,)),
     rs_send=pltpu.SemaphoreType.DMA((54,)),
     rs_recv=pltpu.SemaphoreType.DMA((54,)),
+    ring_send=pltpu.SemaphoreType.DMA((36,)),
+    ring_recv=pltpu.SemaphoreType.DMA((36,)),
     core_send=pltpu.SemaphoreType.DMA((6,)),
     core_recv=pltpu.SemaphoreType.DMA((6,)),
 )
@@ -562,13 +566,70 @@
 
             loop(size // step_of, add)
 
+    def region(order, step):
+        base = 0
+        for k in range(step):
+            base = base + place[order[k]] * (16 >> (2 * k))
+        return base, 16 >> (2 * step)
+
+    def ring(buf, via, recv, step):
+        out = []
+        for p, order in enumerate(ORDERS):
+            base, size = region(order, step)
+            half = size // 2
+            axis = order[step]
+            up, opposite, down = [base + lax.rem(place[axis] + k, 4) * size for k in (1, 2, 3)]
+            ends = along(axis, 1), along(axis, 3)
+            moves = (
+                (opposite, via.at[p, 0], 0), (opposite + half, via.at[p, 1], 1),
+                (up + half, recv.at[p, 0, pl.ds(half, half)], 0), (down, recv.at[p, 1, pl.ds(0, half)], 1),
+                (up, recv.at[p, 0, pl.ds(0, half)], 0), (down + half, recv.at[p, 1, pl.ds(half, half)], 1))
+            out.append([pltpu.make_async_remote_copy(
+                src_ref=buf.at[p, pl.ds(start, half)], dst_ref=target,
+                send_sem=R.ring_send.at[(step * 3 + p) * 6 + n], recv_sem=R.ring_recv.at[(step * 3 + p) * 6 + n],
+                device_id=ends[way], device_id_type=MESH) for n, (start, target, way) in enumerate(moves)])
+        return out
+
+    def ring_start(*what):
+        copies = ring(*what)
+        for pair in (slice(0, 2), slice(2, 4)):
+            for part in copies:
+                for c in part[pair]:
+                    c.start()
+
+    def ring_relay(buf, via, recv, step):
+        copies = ring(buf, via, recv, step)
+        for p, order in enumerate(ORDERS):
+            base, size = region(order, step)
+            half = size // 2
+            up, down = [base + lax.rem(place[order[step]] + k, 4) * size for k in (1, 3)]
+            for way, start in ((0, up), (1, down + half)):
+                copies[p][way].wait_recv()
+                at = pl.ds(start, half)
+                buf[p, at] = (buf[p, at].astype(F32) + via[p, way].astype(F32)).astype(BF)
+                copies[p][4 + way].start()
+
+    def ring_finish(buf, via, recv, step):
+        copies = ring(buf, via, recv, step)
+        for p, order in enumerate(ORDERS):
+            for n, c in enumerate(copies[p]):
+                c.wait_send()
+                if n >= 2:
+                    c.wait_recv()
+            base, size = region(order, step + 1)[0], region(order, step)[1]
+            at = pl.ds(base, size)
+            t = buf[p, at].astype(F32) + recv[p, 0].astype(F32) + recv[p, 1].astype(F32)
+            buf[p, at] = t.astype(BF)
+
     def rs_last(buf, recv, p, copies):
         order = ORDERS[p]
         base = (place[order[0]] * 4 + place[order[1]]) * 4 + place[order[2]]
         t = buf[p, base].astype(F32) + recv[p, 0, 0].astype(F32)
         return t + recv[p, 1, 0].astype(F32) + recv[p, 2, 0].astype(F32)
 
-    big = rs_start(R.b2, R.b2r0, 0, 0)
+    first_ring = (R.b2, R.b2v0, R.b2r0, 0)
+    second_ring = (R.b2, R.b2v1, R.b2r1, 1)
+    ring_start(*first_ring)
     R.mats[...] = take("s4", 0, 608, 576)
     R.matr[...] = take("r3", 0, 576, 608)
 
@@ -588,6 +649,7 @@
         for w in range(4):
             for part in range(3):
                 R.dqkv1[window(w), at(part, pair, 512)] = back[part][w]
+        pl.when(pair == 1)(lambda: ring_relay(*first_ring))
 
     loop(4, bwd1)
 
@@ -615,8 +677,8 @@
         to_core(t).start()
 
     loop(4, term1)
-    rs_add(R.b2, R.b2r0, 0, big)
-    big = rs_start(R.b2, R.b2r1, 0, 1)
+    ring_finish(*first_ring)
+    ring_start(*second_ring)
 
     for t in range(4):
         to_core(t).wait()
@@ -628,6 +690,7 @@
                 R.b1[p, block] = g[n].astype(BF)
     mine = R.b1
     small = rs_start(mine, R.b1r0, 27, 0)
+    ring_relay(*second_ring)
 
     def grad_rolled1(n):
         R.gm1[:, tile(n)] = nt(R.dqkv1[...], R.w1[tile(n), :]).astype(BF)
@@ -651,7 +714,7 @@
     R.matr[...] = take("r4", 0, 576, 608)
     rs_add(mine, R.b1r0, 0, small)
     small = rs_start(mine, R.b1r1, 27, 1)
-    rs_add(R.b2, R.b2r1, 1, big)
+    ring_finish(*second_ring)
     big = rs_start(R.b2, R.b2r2, 0, 2)
     wait(halo_r)
     R.v_res[...] = nn(take("rr", 0, CELLS, 192), R.cr[1]).astype(BF).reshape(72, 2, 1024)

time: 87.5 us -> 86.1 us (0.984)
  Pallas kernels: 86.5 us -> 84.4 us
    pallas_call x1, Pallas kernels: 84.5 us -> 82.3 us  [shards(): pl.pallas_call(functools.partial(body, sizes), out_shape=shapes, in_specs...]
where the time goes in v5:
time: 86.1 us; the launch traced here: 85.2 us
  Pallas kernels  84.4 us (98%)
    pallas_call x1, Pallas kernels, shards(): pl.pallas_call(functools.partial(body, sizes), out_shape=shapes, in_specs...  82.3 us
    pallas_call x1, Pallas kernels, shards(): pl.pallas_call(hand_on, out_shape=shapes, in_specs=[pl.BlockSpec(memory_s...  2.07 us

profile of v5, /device:TPU:0, one launch (start us, length us, event | category | flops | bytes accessed | tf_op | source)
XLA Modules:
  0.0 85.2 jit_solution(5977559745302286643)
XLA Ops:
  0.6 82.3 %shard_map.165 = (bf16[72,2,1024]{2,1,0:T(2,128)(2,1)}, bf16[576,512]{1,0:T(8,128)(2,1)}, f32[32,192]{1,0:T(8,128)}, f32[64,384]{1,0:T(8,128)}) custom-call(bf16[576,512]{1,0:T(8,128)(2,1)} %bitcast.16, bf16[72,2,1024]{2,1,0:T(2,128)(2,1)} %bitcast.18, bf16[512,1536]{1,0:T(8,128)(2,1)} %refs_2_.1, bf16[512,512]{1,0:T(8,128)(2,1)} %refs_3_.1, ...), custom_call_target="tpu_custom_call" | custom-call | flops 8999999488 | bytes 24000000 | tf_op jit(solution)/shard_map/pallas_call | solution.py:773
  82.9 2.1 %shard_map.166 = (bf16[72,2,1024]{2,1,0:T(2,128)(2,1)}, bf16[576,512]{1,0:T(8,128)(2,1)}, f32[32,192]{1,0:T(8,128)}, f32[64,384]{1,0:T(8,128)}) custom-call(bf16[72,2,1024]{2,1,0:T(2,128)(2,1)} %get-tuple-element.12.refs_0_, bf16[576,512]{1,0:T(8,128)(2,1)} %get-tuple-element.13.refs_1_, f32[32,192]{1,0:T(8,128)} %get-tuple-element.14.refs_2_, ...), custom_call_target="tpu_custom_call" | custom-call | tf_op jit(solution)/shard_map/pallas_call | solution.py:783

commit v6 on v5

--- a/solution.py
+++ b/solution.py
@@ -17,6 +17,7 @@
 HALF = 72
 
 SEG1 = ((0, 336), (336, 112), (448, 112), (560, 48))
+HERE, AWAY, ALL = pl.ds(0, 336), pl.ds(336, 272), pl.ds(0, 576)
 SEG2 = ((0, 48), (48, 48), (96, 48), (144, 48))
 
 
@@ -139,6 +140,7 @@
     shifted=pltpu.VMEM((1152, 768), F32),
     ext=pltpu.VMEM((24, 24, 264), F32),
     bias=pltpu.VMEM((12, CELLS, 288), F32),
+    seen=pltpu.VMEM((576, 1), F32),
     madd=pltpu.VMEM((CELLS, 288), F32),
     xr=pltpu.VMEM((4, 608, 512), BF),
     xs=pltpu.VMEM((4, 272, 512), BF),
@@ -184,7 +186,7 @@
     b1r0=pltpu.VMEM((3, 3, 16, 16, 128), BF),
     b1r1=pltpu.VMEM((3, 3, 4, 16, 128), BF),
     b1r2=pltpu.VMEM((3, 3, 1, 16, 128), BF),
-    load_sem=pltpu.SemaphoreType.DMA((len(LOADS),)),
+    load_sem=pltpu.SemaphoreType.DMA((4 * len(LOADS),)),
     halo_send=pltpu.SemaphoreType.DMA((18,)),
     halo_recv=pltpu.SemaphoreType.DMA((18,)),
     rs_send=pltpu.SemaphoreType.DMA((54,)),
@@ -226,11 +228,20 @@
         at[axis] = lax.rem(at[axis] + k, 4)
         return device(**at)
 
+    def wait(copies):
+        for c in copies:
+            c.wait()
+
     loads = SimpleNamespace()
     for n, name in enumerate(LOADS):
-        copy = pltpu.make_async_copy(getattr(R, "in_" + name), getattr(R, name), R.load_sem.at[n])
-        copy.start()
-        setattr(loads, name, copy)
+        source, target = getattr(R, "in_" + name), getattr(R, name)
+        cuts = 4 if source.shape[0] >= 1024 else 1
+        size = source.shape[0] // cuts
+        pieces = [pltpu.make_async_copy(source.at[pl.ds(c * size, size)], target.at[pl.ds(c * size, size)],
+                                        R.load_sem.at[4 * n + c]) for c in range(cuts)]
+        for copy in pieces:
+            copy.start()
+        setattr(loads, name, pieces)
 
     barrier = pltpu.get_barrier_semaphore()
     partners = list(ahead) + list(behind) + [other]
@@ -256,15 +267,30 @@
             c.start()
         return copies
 
-    def wait(copies):
-        for c in copies:
-            c.wait()
-
     def take(key, start, size, columns):
         n = list(INDEX).index(key)
         col = R.in_index[pl.ds(start, size), n:n + 1]
         hit = col == lax.broadcasted_iota(jnp.int32, (size, columns), 1)
         return jnp.where(hit, 1.0, 0.0).astype(BF)
+
+    def window(w):
+        return pl.ds(pl.multiple_of(w * CELLS, 16), CELLS)
+
+    def tile(n, size=256):
+        return pl.ds(pl.multiple_of(n * size, size), size)
+
+    def fill(ref, key, rows, columns):
+        def some(n):
+            at = tile(n, 32)
+            ref[at, :] = take(key, pl.multiple_of(n * 32, 32), 32, columns)
+
+        loop(rows // 32, some)
+
+    def permute(out, rows, mat, source):
+        def some(n):
+            out[:, tile(n)] = nn(mat[rows, :], source[:, tile(n)]).astype(BF)
+
+        loop(source.shape[1] // 256, some)
 
     def put(n, name):
         copy = pltpu.make_async_copy(getattr(R, "v_" + name), getattr(R, "o_" + name), R.out_sem.at[n])
@@ -278,10 +304,10 @@
     per = nn(jnp.where(row // 24 == col, 1.0, 0.0).astype(BF), seen)
     present = jnp.sum(jnp.where(lax.rem(row, 24) == col, per, 0.0), axis=-1, keepdims=True) > 0.5
 
-    R.mats[...] = take("s1", 0, 608, 576)
-    loads.first.wait()
+    fill(R.mats, "s1", 608, 576)
+    wait(loads.first)
     R.first[...] = jnp.where(present, R.first[...].astype(F32), R.in_mask[...].astype(BF).astype(F32)).astype(BF)
-    R.xs[0] = nn(R.mats[336:, :], R.first[...]).astype(BF)
+    permute(R.xs.at[0], AWAY, R.mats, R.first)
 
     R.tables[...] = jnp.zeros((24, 768), F32)
     R.tables[0:8, 0:759] = R.in_table1[...]
@@ -296,14 +322,14 @@
 
     pl.semaphore_wait(barrier, len(partners))
     halo0 = exchange(0, SEG1, R.xs.at[0], R.xr.at[0], behind)
-    R.xr[0, 0:336] = nn(R.mats[0:336, :], R.first[...]).astype(BF)
-    loads.cot.wait()
+    permute(R.xr.at[0, pl.ds(0, 336)], HERE, R.mats, R.first)
+    wait(loads.cot)
     cot = R.cot[...].reshape(CELLS, 1024)
     R.cs[0] = nn(take("sc", 48, 144, CELLS), cot).astype(BF)
     halo_c = exchange(4, SEG2, R.cs.at[0], R.cr.at[0], behind)
     R.cr[0, 0:48] = nn(take("sc", 0, 48, CELLS), cot).astype(BF)
-    R.matr[...] = take("r1", 0, 576, 608)
-    R.mats[...] = take("s2", 0, 608, 576)
+    fill(R.matr, "r1", 576, 608)
+    fill(R.mats, "s2", 608, 576)
 
     def extend(first, heads):
         part = jnp.concatenate([parts[24 * k + first:24 * k + first + heads] for k in range(3)], axis=0)
@@ -313,11 +339,14 @@
                 moved = pltpu.roll(part, (768 - shift) % 768, 1) if shift else part
                 at = (v * 12 + l) * 3 * heads
                 R.shifted[at:at + 3 * heads] = moved
-        got = nn(R.shifted[0:72 * heads].astype(BF), picked)
-        for n in range(24):
-            at = n * 3 * heads
-            R.ext[first:first + heads, n, :] = (
-                got[at:at + heads] + got[at + heads:at + 2 * heads] + got[at + 2 * heads:at + 3 * heads])
+        def some(v):
+            got = nn(R.shifted[tile(v, 24 * heads)].astype(BF), picked)
+            for n in range(8):
+                at = n * 3 * heads
+                R.ext[first:first + heads, v * 8 + n, :] = (
+                    got[at:at + heads] + got[at + heads:at + 2 * heads] + got[at + 2 * heads:at + 3 * heads])
+
+        loop(3, some)
 
     extend(0, 8)
     rows = lax.broadcasted_iota(jnp.int32, (CELLS, CELLS), 0)
@@ -371,22 +400,13 @@
     gain1 = R.in_gain1[...]
     wait(halo0)
 
-    def window(w):
-        return pl.ds(pl.multiple_of(w * CELLS, 16), CELLS)
-
-    def tile(n, size=256):
-        return pl.ds(pl.multiple_of(n * size, size), size)
-
-    def place1(n):
-        R.x1[:, tile(n)] = nn(R.matr[...], R.xr[0, :, tile(n)]).astype(BF)
-
     def norm1(w):
         dev, inv = norm_stats(R.x1[window(w), :].astype(F32))
         R.rolled1[window(w), :] = (dev * inv * gain1).astype(BF)
 
-    loop(2, place1)
+    permute(R.x1, ALL, R.matr, R.xr.at[0])
     loop(4, norm1)
-    loads.w1.wait()
+    wait(loads.w1)
 
     def qkv1(n):
         c = pl.ds(pl.multiple_of(n * 256, 256), 256)
@@ -409,7 +429,7 @@
             R.mixed1[window(w), at(0, pair, 512)] = o[w]
 
     loop(4, fwd1)
-    loads.p1.wait()
+    wait(loads.p1)
 
     def proj1(n):
         branch = nn(R.mixed1[...], R.p1[:, tile(n)]).astype(BF).astype(F32)
@@ -417,16 +437,16 @@
 
     loop(2, proj1)
 
-    R.xs[1] = nn(R.mats[336:, :], R.out1[...]).astype(BF)
+    permute(R.xs.at[1], AWAY, R.mats, R.out1)
     halo1 = exchange(1, SEG1, R.xs.at[1], R.xr.at[1], behind)
-    R.xr[1, 0:336] = nn(R.mats[0:336, :], R.out1[...]).astype(BF)
+    permute(R.xr.at[1, pl.ds(0, 336)], HERE, R.mats, R.out1)
     extend(8, 16)
     loop(8, expand_masked)
-    R.mats[...] = take("s3", 0, 608, 576)
-    R.matr[...] = take("r2", 0, 576, 608)
+    fill(R.mats, "s3", 608, 576)
+    fill(R.matr, "r2", 576, 608)
     wait(halo_c)
     R.ct[...] = nn(take("rc", 0, CELLS, 192), R.cr[0]).astype(BF)
-    loads.p2.wait()
+    wait(loads.p2)
 
     def grad_mixed2(n):
         c = pl.ds(pl.multiple_of(n * 256, 256), 256)
@@ -435,18 +455,21 @@
     loop(4, grad_mixed2)
     R.rolled1t[...] = R.rolled1[...].T
     wait(halo1)
-    R.merged[...] = nn(R.matr[...], R.xr[1]).astype(BF)
-    loads.wm.wait()
-    acc = nn(R.merged[0:CELLS, :], R.wm[0:512, :])
-    for s in range(1, 4):
-        acc = acc + nn(R.merged[s * CELLS:(s + 1) * CELLS, :], R.wm[s * 512:(s + 1) * 512, :])
-    second = acc.astype(BF)
-    R.second[...] = second
+    permute(R.merged, ALL, R.matr, R.xr.at[1])
+    wait(loads.wm)
+    def merge(n):
+        acc = nn(R.merged[0:CELLS, :], R.wm[0:512, tile(n)])
+        for s in range(1, 4):
+            acc = acc + nn(R.merged[s * CELLS:(s + 1) * CELLS, :], R.wm[s * 512:(s + 1) * 512, tile(n)])
+        R.second[:, tile(n)] = acc.astype(BF)
+
+    loop(4, merge)
+    second = R.second[...]
     gain2 = R.in_gain2[...]
     dev, inv = norm_stats(second.astype(F32))
     rolled2 = (dev * inv * gain2).astype(BF)
     R.rolled2[...] = rolled2
-    loads.w2.wait()
+    wait(loads.w2)
 
     def qkv2(n):
         c = pl.ds(pl.multiple_of(n * 512, 512), 512)
@@ -485,9 +508,10 @@
         recv_sem=R.core_recv.at[1], device_id=other, device_id_type=MESH)
     core1.start()
 
-    grad_rolled = nt(R.dqkv2[0, :, 0:1024], R.w2[:, 0:1024])
-    grad_rolled = grad_rolled + nt(R.dqkv2[0, :, 1024:2048], R.w2[:, 1024:2048])
-    grad_rolled = grad_rolled + nt(R.dqkv2[0, :, 2048:3072], R.w2[:, 2048:3072])
+    def grad_rolled2(n):
+        R.gm2[:, tile(n)] = nt(R.dqkv2[0], R.w2[tile(n), :]).astype(BF)
+
+    loop(4, grad_rolled2)
 
     def norm_back(grad, xin, gain, grad_out):
         grad = grad.astype(BF).astype(F32) * gain
@@ -497,12 +521,15 @@
                        - hat * jnp.mean(grad * hat, axis=-1, keepdims=True))
         return (grad_out.astype(F32) + inner.astype(BF).astype(F32)).astype(BF)
 
-    R.gs[...] = norm_back(grad_rolled, R.second[...], gain2, R.ct[...])
-    for s in range(4):
-        R.merged[s * CELLS:(s + 1) * CELLS, :] = nt(R.gs[...], R.wm[s * 512:(s + 1) * 512, :]).astype(BF)
-    R.xs[2] = nn(R.mats[336:, :], R.merged[...]).astype(BF)
+    R.gs[...] = norm_back(R.gm2[...], R.second[...], gain2, R.ct[...])
+
+    def unmerge(s):
+        R.merged[window(s), :] = nt(R.gs[...], R.wm[tile(s, 512), :]).astype(BF)
+
+    loop(4, unmerge)
+    permute(R.xs.at[2], AWAY, R.mats, R.merged)
     halo2 = exchange(2, SEG1, R.xs.at[2], R.xr.at[2], ahead)
-    R.xr[2, 0:336] = nn(R.mats[0:336, :], R.merged[...]).astype(BF)
+    permute(R.xr.at[2, pl.ds(0, 336)], HERE, R.mats, R.merged)
 
     R.halft[0] = R.half2[core].T
     core0.wait()
@@ -605,8 +632,12 @@
             up, down = [base + lax.rem(place[order[step]] + k, 4) * size for k in (1, 3)]
             for way, start in ((0, up), (1, down + half)):
                 copies[p][way].wait_recv()
-                at = pl.ds(start, half)
-                buf[p, at] = (buf[p, at].astype(F32) + via[p, way].astype(F32)).astype(BF)
+
+                def add(n):
+                    at = pl.ds(start + n * 2, 2)
+                    buf[p, at] = (buf[p, at].astype(F32) + via[p, way, pl.ds(n * 2, 2)].astype(F32)).astype(BF)
+
+                loop(half // 2, add)
                 copies[p][4 + way].start()
 
     def ring_finish(buf, via, recv, step):
@@ -617,9 +648,13 @@
                 if n >= 2:
                     c.wait_recv()
             base, size = region(order, step + 1)[0], region(order, step)[1]
-            at = pl.ds(base, size)
-            t = buf[p, at].astype(F32) + recv[p, 0].astype(F32) + recv[p, 1].astype(F32)
-            buf[p, at] = t.astype(BF)
+
+            def add(n):
+                at, near = pl.ds(base + n * 2, 2), pl.ds(n * 2, 2)
+                t = buf[p, at].astype(F32) + recv[p, 0, near].astype(F32) + recv[p, 1, near].astype(F32)
+                buf[p, at] = t.astype(BF)
+
+            loop(size // 2, add)
 
     def rs_last(buf, recv, p, copies):
         order = ORDERS[p]
@@ -630,11 +665,11 @@
     first_ring = (R.b2, R.b2v0, R.b2r0, 0)
     second_ring = (R.b2, R.b2v1, R.b2r1, 1)
     ring_start(*first_ring)
-    R.mats[...] = take("s4", 0, 608, 576)
-    R.matr[...] = take("r3", 0, 576, 608)
+    fill(R.mats, "s4", 608, 576)
+    fill(R.matr, "r3", 576, 608)
 
     wait(halo2)
-    R.g1[...] = nn(R.matr[...], R.xr[2]).astype(BF)
+    permute(R.g1, ALL, R.matr, R.xr.at[2])
 
     def grad_mixed1(n):
         R.gm1[:, tile(n)] = nt(R.g1[...], R.p1[tile(n), :]).astype(BF)
@@ -680,7 +715,7 @@
     ring_finish(*first_ring)
     ring_start(*second_ring)
 
-    for t in range(4):
+    def add_core(t):
         to_core(t).wait()
         for p, order in enumerate(ORDERS):
             g = R.b1h[t, core, p].astype(F32) + R.b1c[t, p].astype(F32)
@@ -688,6 +723,8 @@
                 at = dict(z=n // 4, x=n % 4, y=t)
                 block = (at[order[0]] * 4 + at[order[1]]) * 4 + at[order[2]]
                 R.b1[p, block] = g[n].astype(BF)
+
+    loop(4, add_core)
     mine = R.b1
     small = rs_start(mine, R.b1r0, 27, 0)
     ring_relay(*second_ring)
@@ -701,17 +738,20 @@
 
     loop(2, grad_rolled1)
     loop(4, tail1)
-    R.xs[3] = nn(R.mats[336:, :], R.out1[...]).astype(BF)
+    permute(R.xs.at[3], AWAY, R.mats, R.out1)
     halo3 = exchange(3, SEG1, R.xs.at[3], R.xr.at[3], ahead)
-    R.xr[3, 0:336] = nn(R.mats[0:336, :], R.out1[...]).astype(BF)
-
-    branch = nn(R.mixed2[...], R.p2[...]).astype(BF).astype(F32)
-    R.res[...] = (R.second[...].astype(F32) + branch).astype(BF)
+    permute(R.xr.at[3, pl.ds(0, 336)], HERE, R.mats, R.out1)
+
+    def proj2(n):
+        branch = nn(R.mixed2[...], R.p2[:, tile(n)]).astype(BF).astype(F32)
+        R.res[:, tile(n)] = (R.second[:, tile(n)].astype(F32) + branch).astype(BF)
+
+    loop(4, proj2)
     R.cs[1] = nn(take("sr", 48, 144, CELLS), R.res[...]).astype(BF)
     halo_r = exchange(5, SEG2, R.cs.at[1], R.cr.at[1], ahead)
     R.cr[1, 0:48] = nn(take("sr", 0, 48, CELLS), R.res[...]).astype(BF)
 
-    R.matr[...] = take("r4", 0, 576, 608)
+    fill(R.matr, "r4", 576, 608)
     rs_add(mine, R.b1r0, 0, small)
     small = rs_start(mine, R.b1r1, 27, 1)
     ring_finish(*second_ring)
@@ -722,7 +762,12 @@
     rs_add(mine, R.b1r1, 1, small)
     small = rs_start(mine, R.b1r2, 27, 2)
     wait(halo3)
-    R.v_tok[...] = jnp.where(present, nn(R.matr[...], R.xr[3]), 0.0).astype(BF)
+    R.seen[...] = jnp.where(present, 1.0, 0.0).astype(F32)
+
+    def final(n):
+        R.v_tok[:, tile(n)] = (nn(R.matr[...], R.xr[3, :, tile(n)]) * R.seen[...]).astype(BF)
+
+    loop(2, final)
     puts.append(put(1, "tok"))
     wait(big)
     for p in range(3):

time: 86.1 us -> 91.1 us (1.058)
  Pallas kernels: 84.4 us -> 90 us
    pallas_call x1, Pallas kernels: 82.3 us -> 87.9 us  [shards(): pl.pallas_call(functools.partial(body, sizes), out_shape=shapes, in_specs...]
where the time goes in v6:
time: 91.1 us; the launch traced here: 90.8 us
  Pallas kernels  90 us (99%)
    pallas_call x1, Pallas kernels, shards(): pl.pallas_call(functools.partial(body, sizes), out_shape=shapes, in_specs...  87.9 us
    pallas_call x1, Pallas kernels, shards(): pl.pallas_call(hand_on, out_shape=shapes, in_specs=[pl.BlockSpec(memory_s...  2.07 us

profile of v6, /device:TPU:0, one launch (start us, length us, event | category | flops | bytes accessed | tf_op | source)
XLA Modules:
  0.0 90.8 jit_solution(10900233655068826925)
XLA Ops:
  0.6 87.9 %shard_map.165 = (bf16[72,2,1024]{2,1,0:T(2,128)(2,1)}, bf16[576,512]{1,0:T(8,128)(2,1)}, f32[32,192]{1,0:T(8,128)}, f32[64,384]{1,0:T(8,128)}) custom-call(bf16[576,512]{1,0:T(8,128)(2,1)} %bitcast.16, bf16[72,2,1024]{2,1,0:T(2,128)(2,1)} %bitcast.18, bf16[512,1536]{1,0:T(8,128)(2,1)} %refs_2_.1, bf16[512,512]{1,0:T(8,128)(2,1)} %refs_3_.1, ...), custom_call_target="tpu_custom_call" | custom-call | flops 8999999488 | bytes 24000000 | tf_op jit(solution)/shard_map/pallas_call | solution.py:818
  88.6 2.1 %shard_map.166 = (bf16[72,2,1024]{2,1,0:T(2,128)(2,1)}, bf16[576,512]{1,0:T(8,128)(2,1)}, f32[32,192]{1,0:T(8,128)}, f32[64,384]{1,0:T(8,128)}) custom-call(bf16[72,2,1024]{2,1,0:T(2,128)(2,1)} %get-tuple-element.12.refs_0_, bf16[576,512]{1,0:T(8,128)(2,1)} %get-tuple-element.13.refs_1_, f32[32,192]{1,0:T(8,128)} %get-tuple-element.14.refs_2_, ...), custom_call_target="tpu_custom_call" | custom-call | tf_op jit(solution)/shard_map/pallas_call | solution.py:828

commit v7 on v5

--- a/solution.py
+++ b/solution.py
@@ -127,8 +127,13 @@
     return dev, lax.rsqrt(spread + EPS)
 
 
+def aligned(start, multiple):
+    return start if isinstance(start, int) else pl.multiple_of(start, multiple)
+
+
 def loop(n, body):
-    lax.fori_loop(0, n, lambda i, c: (body(i), c)[1], 0)
+    for i in range(n):
+        body(i)
 
 
 SCRATCH = dict(
@@ -347,7 +352,7 @@
         return jnp.concatenate([t * left, t * right], axis=0)
 
     def at(part, pair, width):
-        return pl.ds(pl.multiple_of(part * width + pair * 128, 128), 128)
+        return pl.ds(aligned(part * width + pair * 128, 128), 128)
 
     def heads_of(t):
         return jnp.where(is_left, t[:CELLS], t[CELLS:])
@@ -372,10 +377,10 @@
     wait(halo0)
 
     def window(w):
-        return pl.ds(pl.multiple_of(w * CELLS, 16), CELLS)
+        return pl.ds(aligned(w * CELLS, 16), CELLS)
 
     def tile(n, size=256):
-        return pl.ds(pl.multiple_of(n * size, size), size)
+        return pl.ds(aligned(n * size, size), size)
 
     def place1(n):
         R.x1[:, tile(n)] = nn(R.matr[...], R.xr[0, :, tile(n)]).astype(BF)
@@ -389,7 +394,7 @@
     loads.w1.wait()
 
     def qkv1(n):
-        c = pl.ds(pl.multiple_of(n * 256, 256), 256)
+        c = pl.ds(aligned(n * 256, 256), 256)
         R.qkv1[:, c] = nn(R.rolled1[...], R.w1[:, c]).astype(BF)
 
     loop(6, qkv1)
@@ -429,7 +434,7 @@
     loads.p2.wait()
 
     def grad_mixed2(n):
-        c = pl.ds(pl.multiple_of(n * 256, 256), 256)
+        c = pl.ds(aligned(n * 256, 256), 256)
         R.gm2[:, c] = nt(R.ct[...], R.p2[c, :]).astype(BF)
 
     loop(4, grad_mixed2)
@@ -449,7 +454,7 @@
     loads.w2.wait()
 
     def qkv2(n):
-        c = pl.ds(pl.multiple_of(n * 512, 512), 512)
+        c = pl.ds(aligned(n * 512, 512), 512)
         R.qkv2[:, c] = nn(R.rolled2[...], R.w2[:, c]).astype(BF)
 
     loop(6, qkv2)
@@ -649,7 +654,8 @@
         for w in range(4):
             for part in range(3):
                 R.dqkv1[window(w), at(part, pair, 512)] = back[part][w]
-        pl.when(pair == 1)(lambda: ring_relay(*first_ring))
+        if pair == 1:
+            ring_relay(*first_ring)
 
     loop(4, bwd1)
 
@@ -659,7 +665,7 @@
             recv_sem=R.core_recv.at[2 + t], device_id=other, device_id_type=MESH)
 
     def term1(t):
-        c = pl.ds(pl.multiple_of(t * 384, 128), 384)
+        c = pl.ds(aligned(t * 384, 128), 384)
         g = nn(R.rolled1t[...], R.dqkv1[:, c])
         pick = is_left[0:16]
         for zz in range(4):

time: 86.1 us -> 79.8 us (0.927)
  Pallas kernels: 84.4 us -> 78.3 us
    pallas_call x1, Pallas kernels: 82.3 us -> 76.2 us  [shards(): pl.pallas_call(functools.partial(body, sizes), out_shape=shapes, in_specs...]
where the time goes in v7:
time: 79.8 us; the launch traced here: 79.1 us
  Pallas kernels  78.3 us (98%)
  between operations  0.82 us (1%)
    pallas_call x1, Pallas kernels, shards(): pl.pallas_call(functools.partial(body, sizes), out_shape=shapes, in_specs...  76.2 us
    pallas_call x1, Pallas kernels, shards(): pl.pallas_call(hand_on, out_shape=shapes, in_specs=[pl.BlockSpec(memory_s...  2.07 us

profile of v7, /device:TPU:0, one launch (start us, length us, event | category | flops | bytes accessed | tf_op | source)
XLA Modules:
  0.0 79.1 jit_solution(10660614252172685722)
XLA Ops:
  0.6 76.2 %shard_map.165 = (bf16[72,2,1024]{2,1,0:T(2,128)(2,1)}, bf16[576,512]{1,0:T(8,128)(2,1)}, f32[32,192]{1,0:T(8,128)}, f32[64,384]{1,0:T(8,128)}) custom-call(bf16[576,512]{1,0:T(8,128)(2,1)} %bitcast.16, bf16[72,2,1024]{2,1,0:T(2,128)(2,1)} %bitcast.18, bf16[512,1536]{1,0:T(8,128)(2,1)} %refs_2_.1, bf16[512,512]{1,0:T(8,128)(2,1)} %refs_3_.1, ...), custom_call_target="tpu_custom_call" | custom-call | flops 8999999488 | bytes 24000000 | tf_op jit(solution)/shard_map/pallas_call | solution.py:779
  76.9 2.1 %shard_map.166 = (bf16[72,2,1024]{2,1,0:T(2,128)(2,1)}, bf16[576,512]{1,0:T(8,128)(2,1)}, f32[32,192]{1,0:T(8,128)}, f32[64,384]{1,0:T(8,128)}) custom-call(bf16[72,2,1024]{2,1,0:T(2,128)(2,1)} %get-tuple-element.12.refs_0_, bf16[576,512]{1,0:T(8,128)(2,1)} %get-tuple-element.13.refs_1_, f32[32,192]{1,0:T(8,128)} %get-tuple-element.14.refs_2_, ...), custom_call_target="tpu_custom_call" | custom-call | tf_op jit(solution)/shard_map/pallas_call | solution.py:789

commit v8 on v7

--- a/solution.py
+++ b/solution.py
@@ -99,13 +99,26 @@
 
 
 INDEX = _indices()
-TABLE_OF = np.full((768, len(INDEX)), -1, np.int32)
-for _n, _rows in enumerate(INDEX.values()):
-    TABLE_OF[:len(_rows), _n] = _rows
-
-SHAPES = dict(first=(576, 512), cot=(72, 2, 1024), w1=(512, 1536), p1=(512, 512), p2=(1024, 1024),
-              wm=(2048, 1024), w2=(1024, 3072))
+COLUMNS = dict(s1=576, r1=608, s2=576, r2=608, s3=576, r3=608, s4=576, r4=608, sc=CELLS, rc=192, sr=CELLS, rr=192,
+               flip=768, pick=264)
+
+
+def _matrix(key):
+    index = np.asarray(INDEX[key])
+    m = np.zeros((len(index), COLUMNS[key]), np.float32)
+    rows = np.nonzero(index >= 0)[0]
+    m[rows, index[rows]] = 1
+    return m.astype(jnp.bfloat16)
+
+
+MATRICES = {k: _matrix(k) for k in INDEX}
+
+SHAPES = dict(first=(576, 512), s1=(608, 576), cot=(72, 2, 1024), sc=(192, CELLS), flip=(768, 768), pick=(768, 264),
+              r1=(576, 608), w1=(512, 1536), p1=(512, 512), rc=(CELLS, 192), p2=(1024, 1024), wm=(2048, 1024),
+              w2=(1024, 3072), sr=(192, CELLS), rr=(CELLS, 192), s2=(608, 576), r2=(576, 608), s3=(608, 576),
+              r3=(576, 608), s4=(608, 576), r4=(576, 608))
 LOADS = tuple(SHAPES)
+LATER = dict(s2="s1", s3="s1", s4="s1", r2="r1", r3="r1", r4="r1")
 
 
 def nn(a, b):
@@ -137,13 +150,13 @@
 
 
 SCRATCH = dict(
-    {k: pltpu.VMEM(SHAPES[k], BF) for k in LOADS},
-    mats=pltpu.VMEM((608, 576), BF),
-    matr=pltpu.VMEM((576, 608), BF),
+    {k: pltpu.VMEM(SHAPES[k], BF) for k in LOADS if k not in LATER},
     tables=pltpu.VMEM((24, 768), F32),
     shifted=pltpu.VMEM((1152, 768), F32),
     ext=pltpu.VMEM((24, 24, 264), F32),
     bias=pltpu.VMEM((12, CELLS, 288), F32),
+    inv1=pltpu.VMEM((576, 1), F32),
+    hat1=pltpu.VMEM((576, 512), F32),
     madd=pltpu.VMEM((CELLS, 288), F32),
     xr=pltpu.VMEM((4, 608, 512), BF),
     xs=pltpu.VMEM((4, 272, 512), BF),
@@ -199,7 +212,7 @@
     core_send=pltpu.SemaphoreType.DMA((6,)),
     core_recv=pltpu.SemaphoreType.DMA((6,)),
 )
-SMALL = ("index", "seen", "mask", "table1", "table2", "gain1", "gain2")
+SMALL = ("seen", "mask", "table1", "table2", "gain1", "gain2")
 OUTPUTS = ("o_res", "o_tok", "o_q1", "o_q2")
 
 ORDERS = (("z", "x", "y"), ("x", "y", "z"), ("y", "z", "x"))
@@ -233,8 +246,10 @@
 
     loads = SimpleNamespace()
     for n, name in enumerate(LOADS):
-        copy = pltpu.make_async_copy(getattr(R, "in_" + name), getattr(R, name), R.load_sem.at[n])
-        copy.start()
+        target = getattr(R, LATER.get(name, name))
+        copy = pltpu.make_async_copy(getattr(R, "in_" + name), target, R.load_sem.at[n])
+        if name not in LATER:
+            copy.start()
         setattr(loads, name, copy)
 
     barrier = pltpu.get_barrier_semaphore()
@@ -265,12 +280,6 @@
         for c in copies:
             c.wait()
 
-    def take(key, start, size, columns):
-        n = list(INDEX).index(key)
-        col = R.in_index[pl.ds(start, size), n:n + 1]
-        hit = col == lax.broadcasted_iota(jnp.int32, (size, columns), 1)
-        return jnp.where(hit, 1.0, 0.0).astype(BF)
-
     def put(n, name):
         copy = pltpu.make_async_copy(getattr(R, "v_" + name), getattr(R, "o_" + name), R.out_sem.at[n])
         copy.start()
@@ -283,10 +292,21 @@
     per = nn(jnp.where(row // 24 == col, 1.0, 0.0).astype(BF), seen)
     present = jnp.sum(jnp.where(lax.rem(row, 24) == col, per, 0.0), axis=-1, keepdims=True) > 0.5
 
-    R.mats[...] = take("s1", 0, 608, 576)
     loads.first.wait()
     R.first[...] = jnp.where(present, R.first[...].astype(F32), R.in_mask[...].astype(BF).astype(F32)).astype(BF)
-    R.xs[0] = nn(R.mats[336:, :], R.first[...]).astype(BF)
+    loads.s1.wait()
+    R.xs[0] = nn(R.s1[336:, :], R.first[...]).astype(BF)
+
+    pl.semaphore_wait(barrier, len(partners))
+    halo0 = exchange(0, SEG1, R.xs.at[0], R.xr.at[0], behind)
+    R.xr[0, 0:336] = nn(R.s1[0:336, :], R.first[...]).astype(BF)
+    loads.s2.start()
+    loads.sc.wait()
+    loads.cot.wait()
+    cot = R.cot[...].reshape(CELLS, 1024)
+    R.cs[0] = nn(R.sc[48:, :], cot).astype(BF)
+    halo_c = exchange(4, SEG2, R.cs.at[0], R.cr.at[0], behind)
+    R.cr[0, 0:48] = nn(R.sc[0:48, :], cot).astype(BF)
 
     R.tables[...] = jnp.zeros((24, 768), F32)
     R.tables[0:8, 0:759] = R.in_table1[...]
@@ -296,19 +316,10 @@
     mid = (table - high).astype(BF).astype(F32)
     low = table - high - mid
     parts = jnp.concatenate([high, mid, low], axis=0).astype(BF)
-    parts = nn(parts, take("flip", 0, 768, 768))
-    picked = take("pick", 0, 768, 264)
-
-    pl.semaphore_wait(barrier, len(partners))
-    halo0 = exchange(0, SEG1, R.xs.at[0], R.xr.at[0], behind)
-    R.xr[0, 0:336] = nn(R.mats[0:336, :], R.first[...]).astype(BF)
-    loads.cot.wait()
-    cot = R.cot[...].reshape(CELLS, 1024)
-    R.cs[0] = nn(take("sc", 48, 144, CELLS), cot).astype(BF)
-    halo_c = exchange(4, SEG2, R.cs.at[0], R.cr.at[0], behind)
-    R.cr[0, 0:48] = nn(take("sc", 0, 48, CELLS), cot).astype(BF)
-    R.matr[...] = take("r1", 0, 576, 608)
-    R.mats[...] = take("s2", 0, 608, 576)
+    loads.flip.wait()
+    parts = nn(parts, R.flip[...])
+    loads.pick.wait()
+    picked = R.pick[...]
 
     def extend(first, heads):
         part = jnp.concatenate([parts[24 * k + first:24 * k + first + heads] for k in range(3)], axis=0)
@@ -374,6 +385,7 @@
         return gq, gk, gv
 
     gain1 = R.in_gain1[...]
+    loads.r1.wait()
     wait(halo0)
 
     def window(w):
@@ -383,14 +395,17 @@
         return pl.ds(aligned(n * size, size), size)
 
     def place1(n):
-        R.x1[:, tile(n)] = nn(R.matr[...], R.xr[0, :, tile(n)]).astype(BF)
+        R.x1[:, tile(n)] = nn(R.r1[...], R.xr[0, :, tile(n)]).astype(BF)
 
     def norm1(w):
         dev, inv = norm_stats(R.x1[window(w), :].astype(F32))
+        R.inv1[window(w), :] = inv
+        R.hat1[window(w), :] = dev * inv
         R.rolled1[window(w), :] = (dev * inv * gain1).astype(BF)
 
     loop(2, place1)
     loop(4, norm1)
+    loads.r2.start()
     loads.w1.wait()
 
     def qkv1(n):
@@ -422,15 +437,16 @@
 
     loop(2, proj1)
 
-    R.xs[1] = nn(R.mats[336:, :], R.out1[...]).astype(BF)
+    loads.s2.wait()
+    R.xs[1] = nn(R.s1[336:, :], R.out1[...]).astype(BF)
     halo1 = exchange(1, SEG1, R.xs.at[1], R.xr.at[1], behind)
-    R.xr[1, 0:336] = nn(R.mats[0:336, :], R.out1[...]).astype(BF)
+    R.xr[1, 0:336] = nn(R.s1[0:336, :], R.out1[...]).astype(BF)
+    loads.s3.start()
     extend(8, 16)
     loop(8, expand_masked)
-    R.mats[...] = take("s3", 0, 608, 576)
-    R.matr[...] = take("r2", 0, 576, 608)
     wait(halo_c)
-    R.ct[...] = nn(take("rc", 0, CELLS, 192), R.cr[0]).astype(BF)
+    loads.rc.wait()
+    R.ct[...] = nn(R.rc[...], R.cr[0]).astype(BF)
     loads.p2.wait()
 
     def grad_mixed2(n):
@@ -439,8 +455,10 @@
 
     loop(4, grad_mixed2)
     R.rolled1t[...] = R.rolled1[...].T
+    loads.r2.wait()
     wait(halo1)
-    R.merged[...] = nn(R.matr[...], R.xr[1]).astype(BF)
+    R.merged[...] = nn(R.r1[...], R.xr[1]).astype(BF)
+    loads.r3.start()
     loads.wm.wait()
     acc = nn(R.merged[0:CELLS, :], R.wm[0:512, :])
     for s in range(1, 4):
@@ -448,8 +466,9 @@
     second = acc.astype(BF)
     R.second[...] = second
     gain2 = R.in_gain2[...]
-    dev, inv = norm_stats(second.astype(F32))
-    rolled2 = (dev * inv * gain2).astype(BF)
+    dev2, inv2 = norm_stats(second.astype(F32))
+    hat2 = dev2 * inv2
+    rolled2 = (hat2 * gain2).astype(BF)
     R.rolled2[...] = rolled2
     loads.w2.wait()
 
@@ -494,20 +513,20 @@
     grad_rolled = grad_rolled + nt(R.dqkv2[0, :, 1024:2048], R.w2[:, 1024:2048])
     grad_rolled = grad_rolled + nt(R.dqkv2[0, :, 2048:3072], R.w2[:, 2048:3072])
 
-    def norm_back(grad, xin, gain, grad_out):
+    def norm_back(grad, hat, inv, gain, grad_out):
         grad = grad.astype(BF).astype(F32) * gain
-        dev, inv = norm_stats(xin.astype(F32))
-        hat = dev * inv
         inner = inv * (grad - jnp.mean(grad, axis=-1, keepdims=True)
                        - hat * jnp.mean(grad * hat, axis=-1, keepdims=True))
         return (grad_out.astype(F32) + inner.astype(BF).astype(F32)).astype(BF)
 
-    R.gs[...] = norm_back(grad_rolled, R.second[...], gain2, R.ct[...])
+    R.gs[...] = norm_back(grad_rolled, hat2, inv2, gain2, R.ct[...])
     for s in range(4):
         R.merged[s * CELLS:(s + 1) * CELLS, :] = nt(R.gs[...], R.wm[s * 512:(s + 1) * 512, :]).astype(BF)
-    R.xs[2] = nn(R.mats[336:, :], R.merged[...]).astype(BF)
+    loads.s3.wait()
+    R.xs[2] = nn(R.s1[336:, :], R.merged[...]).astype(BF)
     halo2 = exchange(2, SEG1, R.xs.at[2], R.xr.at[2], ahead)
-    R.xr[2, 0:336] = nn(R.mats[0:336, :], R.merged[...]).astype(BF)
+    R.xr[2, 0:336] = nn(R.s1[0:336, :], R.merged[...]).astype(BF)
+    loads.s4.start()
 
     R.halft[0] = R.half2[core].T
     core0.wait()
@@ -635,11 +654,11 @@
     first_ring = (R.b2, R.b2v0, R.b2r0, 0)
     second_ring = (R.b2, R.b2v1, R.b2r1, 1)
     ring_start(*first_ring)
-    R.mats[...] = take("s4", 0, 608, 576)
-    R.matr[...] = take("r3", 0, 576, 608)
-
+
+    loads.r3.wait()
     wait(halo2)
-    R.g1[...] = nn(R.matr[...], R.xr[2]).astype(BF)
+    R.g1[...] = nn(R.r1[...], R.xr[2]).astype(BF)
+    loads.r4.start()
 
     def grad_mixed1(n):
         R.gm1[:, tile(n)] = nt(R.g1[...], R.p1[tile(n), :]).astype(BF)
@@ -664,9 +683,12 @@
             src_ref=R.b1h.at[t, 1 - core], dst_ref=R.b1c.at[t], send_sem=R.core_send.at[2 + t],
             recv_sem=R.core_recv.at[2 + t], device_id=other, device_id_type=MESH)
 
+    wide = []
+
     def term1(t):
-        c = pl.ds(aligned(t * 384, 128), 384)
-        g = nn(R.rolled1t[...], R.dqkv1[:, c])
+        if t % 2 == 0:
+            wide.append(nn(R.rolled1t[...], R.dqkv1[:, tile(t // 2, 768)]))
+        g = wide[-1][:, t % 2 * 384:t % 2 * 384 + 384]
         pick = is_left[0:16]
         for zz in range(4):
             for hh in range(2):
@@ -703,32 +725,35 @@
 
     def tail1(w):
         r = window(w)
-        R.out1[r, :] = norm_back(R.gm1[r, :], R.x1[r, :], gain1, R.g1[r, :])
+        R.out1[r, :] = norm_back(R.gm1[r, :], R.hat1[r, :], R.inv1[r, :], gain1, R.g1[r, :])
 
     loop(2, grad_rolled1)
     loop(4, tail1)
-    R.xs[3] = nn(R.mats[336:, :], R.out1[...]).astype(BF)
+    loads.s4.wait()
+    R.xs[3] = nn(R.s1[336:, :], R.out1[...]).astype(BF)
     halo3 = exchange(3, SEG1, R.xs.at[3], R.xr.at[3], ahead)
-    R.xr[3, 0:336] = nn(R.mats[0:336, :], R.out1[...]).astype(BF)
+    R.xr[3, 0:336] = nn(R.s1[0:336, :], R.out1[...]).astype(BF)
 
     branch = nn(R.mixed2[...], R.p2[...]).astype(BF).astype(F32)
     R.res[...] = (R.second[...].astype(F32) + branch).astype(BF)
-    R.cs[1] = nn(take("sr", 48, 144, CELLS), R.res[...]).astype(BF)
+    loads.sr.wait()
+    R.cs[1] = nn(R.sr[48:, :], R.res[...]).astype(BF)
     halo_r = exchange(5, SEG2, R.cs.at[1], R.cr.at[1], ahead)
-    R.cr[1, 0:48] = nn(take("sr", 0, 48, CELLS), R.res[...]).astype(BF)
-
-    R.matr[...] = take("r4", 0, 576, 608)
+    R.cr[1, 0:48] = nn(R.sr[0:48, :], R.res[...]).astype(BF)
+
     rs_add(mine, R.b1r0, 0, small)
     small = rs_start(mine, R.b1r1, 27, 1)
     ring_finish(*second_ring)
     big = rs_start(R.b2, R.b2r2, 0, 2)
     wait(halo_r)
-    R.v_res[...] = nn(take("rr", 0, CELLS, 192), R.cr[1]).astype(BF).reshape(72, 2, 1024)
+    loads.rr.wait()
+    R.v_res[...] = nn(R.rr[...], R.cr[1]).astype(BF).reshape(72, 2, 1024)
     puts = [put(0, "res")]
     rs_add(mine, R.b1r1, 1, small)
     small = rs_start(mine, R.b1r2, 27, 2)
+    loads.r4.wait()
     wait(halo3)
-    R.v_tok[...] = jnp.where(present, nn(R.matr[...], R.xr[3]), 0.0).astype(BF)
+    R.v_tok[...] = jnp.where(present, nn(R.r1[...], R.xr[3]), 0.0).astype(BF)
     puts.append(put(1, "tok"))
     wait(big)
     for p in range(3):
@@ -768,8 +793,10 @@
     cot = cotangent.transpose(1, 2, 0, 3).reshape(72, 2, 1024)
     seen = observed.transpose(2, 0, 1)
     given = dict(first=first, cot=cot, w1=qkv_one, p1=proj_one, wm=merge_weight, w2=qkv_two, p2=proj_two)
+    for k, m in MATRICES.items():
+        given[k] = jnp.asarray(m)
     args = [given[k] for k in LOADS]
-    args += [jnp.asarray(TABLE_OF), seen, mask_token[None], table_one, table_two, gain_one[None], gain_two[None]]
+    args += [seen, mask_token[None], table_one, table_two, gain_one[None], gain_two[None]]
     shapes = (
         jax.ShapeDtypeStruct((72, 2, 1024), BF),
         jax.ShapeDtypeStruct((576, 512), BF),

time: 79.8 us -> 80.1 us (level)
  no operation moved by 1% of the time
where the time goes in v8:
time: 80.1 us; the launch traced here: 79.3 us
  Pallas kernels  78.5 us (98%)
  between operations  0.82 us (1%)
    pallas_call x1, Pallas kernels, shards(): pl.pallas_call(functools.partial(body, sizes), out_shape=shapes, in_specs...  76.4 us
    pallas_call x1, Pallas kernels, shards(): pl.pallas_call(hand_on, out_shape=shapes, in_specs=[pl.BlockSpec(memory_s...  2.07 us

profile of v8, /device:TPU:0, one launch (start us, length us, event | category | flops | bytes accessed | tf_op | source)
XLA Modules:
  0.0 79.3 jit_solution(14740206878730601293)
XLA Ops:
  0.6 76.4 %shard_map.282 = (bf16[72,2,1024]{2,1,0:T(2,128)(2,1)}, bf16[576,512]{1,0:T(8,128)(2,1)}, f32[32,192]{1,0:T(8,128)}, f32[64,384]{1,0:T(8,128)}) custom-call(bf16[576,512]{1,0:T(8,128)(2,1)} %bitcast.16, bf16[608,576]{1,0:T(8,128)(2,1)} %constant.28.clone.refs_1_, bf16[72,2,1024]{2,1,0:T(2,128)(2,1)} %bitcast.18, bf16[192,144]{1,0:T(8,128)(2,1)} %constant.36.clone.refs_3_, ...), custom_call_target="tpu_custom_call" | custom-call | flops 8999999488 | bytes 24000000 | tf_op jit(solution)/shard_map/pallas_call | solution.py:806
  77.0 2.1 %shard_map.283 = (bf16[72,2,1024]{2,1,0:T(2,128)(2,1)}, bf16[576,512]{1,0:T(8,128)(2,1)}, f32[32,192]{1,0:T(8,128)}, f32[64,384]{1,0:T(8,128)}) custom-call(bf16[72,2,1024]{2,1,0:T(2,128)(2,1)} %get-tuple-element.12.refs_0_, bf16[576,512]{1,0:T(8,128)(2,1)} %get-tuple-element.13.refs_1_, f32[32,192]{1,0:T(8,128)} %get-tuple-element.14.refs_2_, ...), custom_call_target="tpu_custom_call" | custom-call | tf_op jit(solution)/shard_map/pallas_call | solution.py:816

commit v9 on v8

--- a/solution.py
+++ b/solution.py
@@ -385,8 +385,6 @@
         return gq, gk, gv
 
     gain1 = R.in_gain1[...]
-    loads.r1.wait()
-    wait(halo0)
 
     def window(w):
         return pl.ds(aligned(w * CELLS, 16), CELLS)
@@ -394,52 +392,63 @@
     def tile(n, size=256):
         return pl.ds(aligned(n * size, size), size)
 
-    def place1(n):
-        R.x1[:, tile(n)] = nn(R.r1[...], R.xr[0, :, tile(n)]).astype(BF)
+    def span(first, last):
+        return slice(first * CELLS, last * CELLS)
 
     def norm1(w):
-        dev, inv = norm_stats(R.x1[window(w), :].astype(F32))
-        R.inv1[window(w), :] = inv
-        R.hat1[window(w), :] = dev * inv
-        R.rolled1[window(w), :] = (dev * inv * gain1).astype(BF)
-
-    loop(2, place1)
-    loop(4, norm1)
+        rows = span(w, w + 1)
+        dev, inv = norm_stats(R.x1[rows, :].astype(F32))
+        R.inv1[rows, :] = inv
+        R.hat1[rows, :] = dev * inv
+        R.rolled1[rows, :] = (dev * inv * gain1).astype(BF)
+
+    def qkv1(first, last):
+        rows = span(first, last)
+        for n in range(6):
+            R.qkv1[rows, tile(n)] = nn(R.rolled1[rows, :], R.w1[:, tile(n)]).astype(BF)
+
+    def units(which):
+        q2 = [stack(R.qkv1[window(w), at(0, pair, 512)] * BF(0.125)) for pair, w in which]
+        k = [R.qkv1[window(w), at(1, pair, 512)] for pair, w in which]
+        v = [R.qkv1[window(w), at(2, pair, 512)] for pair, w in which]
+        return q2, k, v
+
+    def fwd1(which):
+        bias = [R.bias[pair] + R.madd[...] if w % 2 else R.bias[pair] for pair, w in which]
+        _, pb, o = attend(*units(which), bias)
+        for n, (pair, w) in enumerate(which):
+            R.prob1[pair * 4 + w] = pb[n]
+            R.mixed1[window(w), at(0, pair, 512)] = o[n]
+
+    def proj1(first, last):
+        rows = span(first, last)
+        for n in range(2):
+            branch = nn(R.mixed1[rows, :], R.p1[:, tile(n)]).astype(BF).astype(F32)
+            R.out1[rows, tile(n)] = (R.x1[rows, tile(n)].astype(F32) + branch).astype(BF)
+
+    loads.r1.wait()
+    R.x1[0:CELLS, :] = nn(R.r1[0:CELLS, 0:336], R.xr[0, 0:336, :]).astype(BF)
+    norm1(0)
+    loads.w1.wait()
+    qkv1(0, 1)
+    fwd1([(pair, 0) for pair in range(4)])
+    wait(halo0)
+    R.x1[span(1, 4), :] = nn(R.r1[span(1, 4), :], R.xr[0]).astype(BF)
     loads.r2.start()
-    loads.w1.wait()
-
-    def qkv1(n):
-        c = pl.ds(aligned(n * 256, 256), 256)
-        R.qkv1[:, c] = nn(R.rolled1[...], R.w1[:, c]).astype(BF)
-
-    loop(6, qkv1)
-
-    def four(pair):
-        q2 = [stack(R.qkv1[window(w), at(0, pair, 512)] * BF(0.125)) for w in range(4)]
-        k = [R.qkv1[window(w), at(1, pair, 512)] for w in range(4)]
-        v = [R.qkv1[window(w), at(2, pair, 512)] for w in range(4)]
-        return q2, k, v
-
-    def fwd1(pair):
-        bias = R.bias[pair]
-        masked = bias + R.madd[...]
-        _, pb, o = attend(*four(pair), [bias, masked, bias, masked])
-        for w in range(4):
-            R.prob1[pair * 4 + w] = pb[w]
-            R.mixed1[window(w), at(0, pair, 512)] = o[w]
-
-    loop(4, fwd1)
+    for w in (1, 2, 3):
+        norm1(w)
+    qkv1(1, 4)
+    fwd1([(0, 1), (0, 2), (1, 1), (1, 2)])
+    fwd1([(2, 1), (2, 2), (3, 1), (3, 2)])
     loads.p1.wait()
-
-    def proj1(n):
-        branch = nn(R.mixed1[...], R.p1[:, tile(n)]).astype(BF).astype(F32)
-        R.out1[:, tile(n)] = (R.x1[:, tile(n)].astype(F32) + branch).astype(BF)
-
-    loop(2, proj1)
+    proj1(0, 3)
+    R.out1[span(3, 4), :] = jnp.zeros((CELLS, 512), BF)
 
     loads.s2.wait()
     R.xs[1] = nn(R.s1[336:, :], R.out1[...]).astype(BF)
     halo1 = exchange(1, SEG1, R.xs.at[1], R.xr.at[1], behind)
+    fwd1([(pair, 3) for pair in range(4)])
+    proj1(3, 4)
     R.xr[1, 0:336] = nn(R.s1[0:336, :], R.out1[...]).astype(BF)
     loads.s3.start()
     extend(8, 16)
@@ -655,28 +664,28 @@
     second_ring = (R.b2, R.b2v1, R.b2r1, 1)
     ring_start(*first_ring)
 
+    def back1(which):
+        q2, k, v = units(which)
+        go = [stack(R.gm1[window(w), at(0, pair, 512)]) for pair, w in which]
+        pb = [R.prob1[pair * 4 + w] for pair, w in which]
+        back = attend_back(q2, k, v, [t.astype(F32) for t in pb], pb, go)
+        for n, (pair, w) in enumerate(which):
+            for part in range(3):
+                R.dqkv1[window(w), at(part, pair, 512)] = back[part][n]
+
     loads.r3.wait()
+    R.g1[span(3, 4), :] = nn(R.r1[span(3, 4), 0:336], R.xr[2, 0:336, :]).astype(BF)
+    R.gm1[span(3, 4), :] = nt(R.g1[span(3, 4), :], R.p1[...]).astype(BF)
+    back1([(pair, 3) for pair in range(4)])
     wait(halo2)
-    R.g1[...] = nn(R.r1[...], R.xr[2]).astype(BF)
+    R.g1[span(0, 3), :] = nn(R.r1[span(0, 3), :], R.xr[2]).astype(BF)
     loads.r4.start()
-
-    def grad_mixed1(n):
-        R.gm1[:, tile(n)] = nt(R.g1[...], R.p1[tile(n), :]).astype(BF)
-
-    loop(2, grad_mixed1)
-
-    def bwd1(pair):
-        q2, k, v = four(pair)
-        go = [stack(R.gm1[window(w), at(0, pair, 512)]) for w in range(4)]
-        pb = [R.prob1[pair * 4 + w] for w in range(4)]
-        back = attend_back(q2, k, v, [t.astype(F32) for t in pb], pb, go)
-        for w in range(4):
-            for part in range(3):
-                R.dqkv1[window(w), at(part, pair, 512)] = back[part][w]
+    for n in range(2):
+        R.gm1[span(0, 3), tile(n)] = nt(R.g1[span(0, 3), :], R.p1[tile(n), :]).astype(BF)
+    for pair in range(4):
+        back1([(pair, w) for w in range(3)])
         if pair == 1:
             ring_relay(*first_ring)
-
-    loop(4, bwd1)
 
     def to_core(t):
         return pltpu.make_async_remote_copy(

time: 80.1 us -> 77.6 us (0.969)
  Pallas kernels: 78.5 us -> 75.7 us
    pallas_call x1, Pallas kernels: 76.4 us -> 73.6 us  [shards(): pl.pallas_call(functools.partial(body, sizes), out_shape=shapes, in_specs...]
where the time goes in v9:
time: 77.6 us; the launch traced here: 76.5 us
  Pallas kernels  75.7 us (98%)
  between operations  0.82 us (1%)
    pallas_call x1, Pallas kernels, shards(): pl.pallas_call(functools.partial(body, sizes), out_shape=shapes, in_specs...  73.6 us
    pallas_call x1, Pallas kernels, shards(): pl.pallas_call(hand_on, out_shape=shapes, in_specs=[pl.BlockSpec(memory_s...  2.07 us

profile of v9, /device:TPU:0, one launch (start us, length us, event | category | flops | bytes accessed | tf_op | source)
XLA Modules:
  0.0 76.5 jit_solution(1274205187833737455)
XLA Ops:
  0.6 73.6 %shard_map.282 = (bf16[72,2,1024]{2,1,0:T(2,128)(2,1)}, bf16[576,512]{1,0:T(8,128)(2,1)}, f32[32,192]{1,0:T(8,128)}, f32[64,384]{1,0:T(8,128)}) custom-call(bf16[576,512]{1,0:T(8,128)(2,1)} %bitcast.16, bf16[608,576]{1,0:T(8,128)(2,1)} %constant.28.clone.refs_1_, bf16[72,2,1024]{2,1,0:T(2,128)(2,1)} %bitcast.18, bf16[192,144]{1,0:T(8,128)(2,1)} %constant.36.clone.refs_3_, ...), custom_call_target="tpu_custom_call" | custom-call | flops 8999999488 | bytes 24000000 | tf_op jit(solution)/shard_map/pallas_call | solution.py:815
  74.3 2.1 %shard_map.283 = (bf16[72,2,1024]{2,1,0:T(2,128)(2,1)}, bf16[576,512]{1,0:T(8,128)(2,1)}, f32[32,192]{1,0:T(8,128)}, f32[64,384]{1,0:T(8,128)}) custom-call(bf16[72,2,1024]{2,1,0:T(2,128)(2,1)} %get-tuple-element.12.refs_0_, bf16[576,512]{1,0:T(8,128)(2,1)} %get-tuple-element.13.refs_1_, f32[32,192]{1,0:T(8,128)} %get-tuple-element.14.refs_2_, ...), custom_call_target="tpu_custom_call" | custom-call | tf_op jit(solution)/shard_map/pallas_call | solution.py:825

commit v10 on v9

--- a/solution.py
+++ b/solution.py
@@ -714,8 +714,6 @@
         to_core(t).start()
 
     loop(4, term1)
-    ring_finish(*first_ring)
-    ring_start(*second_ring)
 
     for t in range(4):
         to_core(t).wait()
@@ -727,7 +725,8 @@
                 R.b1[p, block] = g[n].astype(BF)
     mine = R.b1
     small = rs_start(mine, R.b1r0, 27, 0)
-    ring_relay(*second_ring)
+    ring_finish(*first_ring)
+    ring_start(*second_ring)
 
     def grad_rolled1(n):
         R.gm1[:, tile(n)] = nt(R.dqkv1[...], R.w1[tile(n), :]).astype(BF)
@@ -742,6 +741,8 @@
     R.xs[3] = nn(R.s1[336:, :], R.out1[...]).astype(BF)
     halo3 = exchange(3, SEG1, R.xs.at[3], R.xr.at[3], ahead)
     R.xr[3, 0:336] = nn(R.s1[0:336, :], R.out1[...]).astype(BF)
+
+    ring_relay(*second_ring)
 
     branch = nn(R.mixed2[...], R.p2[...]).astype(BF).astype(F32)
     R.res[...] = (R.second[...].astype(F32) + branch).astype(BF)

time: 77.6 us -> 76.4 us (0.985)
  Pallas kernels: 75.7 us -> 74.4 us
    pallas_call x1, Pallas kernels: 73.6 us -> 72.4 us  [shards(): pl.pallas_call(functools.partial(body, sizes), out_shape=shapes, in_specs...]
where the time goes in v10:
time: 76.4 us; the launch traced here: 75.3 us
  Pallas kernels  74.4 us (97%)
  between operations  0.82 us (1%)
    pallas_call x1, Pallas kernels, shards(): pl.pallas_call(functools.partial(body, sizes), out_shape=shapes, in_specs...  72.4 us
    pallas_call x1, Pallas kernels, shards(): pl.pallas_call(hand_on, out_shape=shapes, in_specs=[pl.BlockSpec(memory_s...  2.07 us

profile of v10, /device:TPU:0, one launch (start us, length us, event | category | flops | bytes accessed | tf_op | source)
XLA Modules:
  0.0 75.3 jit_solution(14476294892472572979)
XLA Ops:
  0.6 72.4 %shard_map.282 = (bf16[72,2,1024]{2,1,0:T(2,128)(2,1)}, bf16[576,512]{1,0:T(8,128)(2,1)}, f32[32,192]{1,0:T(8,128)}, f32[64,384]{1,0:T(8,128)}) custom-call(bf16[576,512]{1,0:T(8,128)(2,1)} %bitcast.16, bf16[608,576]{1,0:T(8,128)(2,1)} %constant.28.clone.refs_1_, bf16[72,2,1024]{2,1,0:T(2,128)(2,1)} %bitcast.18, bf16[192,144]{1,0:T(8,128)(2,1)} %constant.36.clone.refs_3_, ...), custom_call_target="tpu_custom_call" | custom-call | flops 8999999488 | bytes 24000000 | tf_op jit(solution)/shard_map/pallas_call | solution.py:816
  73.0 2.1 %shard_map.283 = (bf16[72,2,1024]{2,1,0:T(2,128)(2,1)}, bf16[576,512]{1,0:T(8,128)(2,1)}, f32[32,192]{1,0:T(8,128)}, f32[64,384]{1,0:T(8,128)}) custom-call(bf16[72,2,1024]{2,1,0:T(2,128)(2,1)} %get-tuple-element.12.refs_0_, bf16[576,512]{1,0:T(8,128)(2,1)} %get-tuple-element.13.refs_1_, f32[32,192]{1,0:T(8,128)} %get-tuple-element.14.refs_2_, ...), custom_call_target="tpu_custom_call" | custom-call | tf_op jit(solution)/shard_map/pallas_call | solution.py:826
